TPU v7x, 256 devices: a whole 4x4x8 slice. The times are simulated.
256 devices in a mesh: rep: 8 (over y, core), fsdp: 32 (over z, x).
Axes of the slice: x: 4, y: 4, z: 8, core: 2. Of those that a mesh axis runs over, the one named last changes fastest.
Arguments:
- momentum: float32 [8, 3072, 12288], P('rep', 'fsdp')
- kept: int32 [3072, 192, 4], P('fsdp'), may hold values from 0 to 63, as said below
- counts: int32 [8, 3072, 192], P(None, 'fsdp'), may hold values from 1 to 4, 384 in all within a row
Outputs:
- new_momentum: float32 [8, 3072, 12288], P('rep', 'fsdp')
- update: bfloat16 [3072, 12288], P('fsdp')
Inputs may be any that keep to these rules, and one draw needn't show every extreme that they name: `kept`: the 4 numbers listed for one block are distinct. The counts of one row of one replica sum to 384.
All inputs are finite; a program needn't handle non-finite values.
Results may differ from a plain program's by a relative error of at most 0.001.
Values sent between devices are 32-bit elements; how exact they have to be, the bound alone decides.
No kernel may reach another device: no remote copies, remote signals or barrier semaphores. Data moves between devices by JAX's collectives and lax.ppermute only.
A program may use at most 256 MiB of HBM per device.

v0:
```python
import math

import jax
import jax.numpy as jnp
from jax import lax
from jax.sharding import PartitionSpec as P

CH = 64
KEEP = 4


def paired_table(length):
    width = 2 * length
    row_pos = lax.broadcasted_iota(jnp.int32, (width, width), 0)
    col_pos = lax.broadcasted_iota(jnp.int32, (width, width), 1)
    frequency = (row_pos % length).astype(jnp.float32)
    position = (col_pos % length).astype(jnp.float32)
    waves = jnp.cos(math.pi * (2.0 * position + 1.0) * frequency / (2.0 * length))
    scaling = jnp.where(frequency == 0, math.sqrt(1.0 / length), math.sqrt(2.0 / length))
    same_block = row_pos // length == col_pos // length
    return jnp.where(same_block, waves * scaling, 0.0)


def to_dense(values, kept, freq_ids):
    dense = jnp.zeros(kept.shape[:2] + (CH,), jnp.float32)
    for slot in range(KEEP):
        dense = dense + jnp.where(
            kept[..., slot : slot + 1] == freq_ids, values[..., slot : slot + 1], 0.0
        )
    return dense


def decode(dense_part, basis_pair, row_count, row_width):
    return jnp.dot(
        dense_part.reshape(-1, 2 * CH), basis_pair, precision=lax.Precision.HIGHEST
    ).reshape(row_count, row_width)


def per_device(momentum, kept, counts):
    moment = momentum[0]
    row_count, row_width = moment.shape
    nchunk = row_width // CH
    replicas = lax.axis_size("rep")
    basis_pair = paired_table(CH)
    freq_ids = lax.broadcasted_iota(jnp.int32, (1, 1, CH), 2)
    coeffs = jnp.dot(
        moment.reshape(-1, 2 * CH), basis_pair.T, precision=lax.Precision.HIGHEST
    ).reshape(row_count, nchunk, CH)
    own_counts = lax.dynamic_index_in_dim(counts, lax.axis_index("rep"), 0, keepdims=False)
    slot_shape = kept.shape
    slot_ids = lax.broadcasted_iota(jnp.int32, slot_shape, 2)
    live_slots = slot_ids < own_counts[..., None]
    columns = [
        jnp.sum(jnp.where(kept[..., slot : slot + 1] == freq_ids, coeffs, 0.0), axis=2)
        for slot in range(KEEP)
    ]
    picked = jnp.where(live_slots, jnp.stack(columns, axis=2), 0.0)
    new_moment = moment - decode(to_dense(picked, kept, freq_ids), basis_pair, row_count, row_width)
    slot_vals = lax.all_gather(picked[None], "rep", axis=0, tiled=True)
    coeff_sum = jnp.sum(slot_vals, axis=0)
    raw = decode(to_dense(coeff_sum, kept, freq_ids), basis_pair, row_count, row_width) / replicas
    energy = lax.psum(jnp.sum(raw * raw), "fsdp")
    entries = row_count * row_width * lax.axis_size("fsdp")
    update = (raw * lax.rsqrt(energy / entries + 1e-06)).astype(jnp.bfloat16)
    return (new_moment[None], update)


def solution(mesh):
    placed = (P("rep", "fsdp", None), P("fsdp", None, None), P(None, "fsdp", None))
    return jax.shard_map(
        per_device,
        mesh=mesh,
        in_specs=placed,
        out_specs=(P("rep", "fsdp", None), P("fsdp", None)),
        check_vma=False,
    )
```

profile of v0, /device:TPU:8, one launch (start us, length us, event | category | flops | bytes accessed | tf_op | source)
XLA Modules:
  0.0 265.8 jit_solution(17357505086855595518)
XLA Ops:
  7.2 0.0 copy-start
  7.2 0.0 all-gather.2.cloned.1.call-start
  7.3 1.9 fusion.23
  9.2 5.2 %reshape_squeeze.3 = f32[9216,128]{1,0:T(8,128)} reshape(f32[1,96,12288]{2,1,0:T(8,128)} %param.3) | data formatting | bytes 9437184 | tf_op jit(solution)/shard_map/reshape;squeeze | solution.py:47
  14.4 8.9 %convolution_bitcast_fusion = f32[9216,128]{0,1:T(8,128)} fusion(f32[9216,128]{1,0:T(8,128)} %reshape_squeeze.3, s32[128]{0:T(128)S(1)} %get-tuple-element.25, s32[128]{0:T(128)S(1)} %get-tuple-element.26, s32[128]{0:T(128)S(1)} %get-tuple-element.24, s32[128]{0:T(128)S(1)} %get-tuple-element.27, pred[128]{0:T(512)(128)(4,1)S(1)} %get-tuple-element.22, ...), kind=kOutput, calls=%fused_computation | convolution fusion | flops 1812201472 | bytes 9439488 | tf_op jit(solution)/shard_map/dot_general | solution.py:46
  23.3 6.0 %copy.11 = f32[9216,128]{1,0:T(8,128)} copy(f32[9216,128]{0,1:T(8,128)} %convolution_bitcast_fusion) | data formatting | bytes 9437184 | tf_op jit(solution)/shard_map/dot_general | solution.py:46
  29.4 8.0 %reshape.133 = f32[96,192,64]{2,1,0:T(8,128)} reshape(f32[9216,128]{1,0:T(8,128)} %copy.11) | data formatting | bytes 9437184 | tf_op jit(solution)/shard_map/reshape | solution.py:48
  37.3 0.0 copy-done
  37.4 26.9 %select_reduce_fusion.3 = (f32[96,192]{1,0:T(8,128)S(1)}, f32[96,192]{1,0:T(8,128)S(1)}, f32[96,192]{1,0:T(8,128)S(1)}, f32[96,192]{1,0:T(8,128)S(1)}) fusion(f32[96,192,64]{2,1,0:T(8,128)} %reshape.133, s32[96,192]{1,0:T(8,128)S(1)} %get-tuple-element.31, s32[96,192]{1,0:T(8,128)S(1)} %get-tuple-element.28, s32[96,192]{1,0:T(8,128)S(1)} %get-tuple-element.29, ...), kind=kLoop, calls=%fused_computation.9 | loop fusion | flops 14082048 | bytes 5308416 | tf_op jit(solution)/shard_map/reduce_sum | solution.py:54
  64.3 0.8 maximum_select_fusion.1
  65.0 0.0 all-gather.2.cloned.1.call-update
  65.2 32.2 %all-gather.2.cloned.1.call-done = f32[8,96,192,4]{2,1,3,0:T(8,128)} async-done(((f32[1,96,192,4]{2,1,3,0:T(8,128)}), f32[8,96,192,4]{2,1,3,0:T(8,128)}) %all-gather.2.cloned.1.call-update) | async-done | bytes 2359312 | tf_op jit(solution)/shard_map/all_gather | solution.py:59
  97.4 2.2 reduce_sum.58
  99.6 32.6 %select_add_fusion = (f32[96,192,64]{2,1,0:T(8,128)}, f32[96,192,64]{2,1,0:T(8,128)}) fusion(f32[96,192]{1,0:T(8,128)S(1)} %get-tuple-element.9, f32[96,192]{1,0:T(8,128)S(1)} %get-tuple-element.10, f32[96,192]{1,0:T(8,128)S(1)} %get-tuple-element.11, f32[96,192]{1,0:T(8,128)S(1)} %get-tuple-element.8, s32[96,192]{1,0:T(8,128)S(1)} %get-tuple-element.28, ...), kind=kLoop, calls=%fused_computation.1 | loop fusion | flops 21233664 | bytes 10321920 | tf_op jit(solution)/shard_map/add | solution.py:27
  132.2 8.7 %reshape.136 = f32[9216,128]{1,0:T(8,128)} reshape(f32[96,192,64]{2,1,0:T(8,128)} %get-tuple-element.6) | data formatting | bytes 9437184 | tf_op jit(solution)/shard_map/add | solution.py:27
  140.9 8.4 %multiply_reduce_fusion = (f32[]{:T(128)}, f32[9216,128]{1,0:T(8,128)}) fusion(f32[9216,128]{1,0:T(8,128)} %reshape.136, s32[128]{0:T(128)S(1)} %get-tuple-element.25, s32[128]{0:T(128)S(1)} %get-tuple-element.26, s32[128]{0:T(128)S(1)} %get-tuple-element.24, s32[128]{0:T(128)S(1)} %get-tuple-element.27, pred[128]{0:T(512)(128)(4,1)S(1)} %get-tuple-element.22, ...), kind=kOutput, calls=%fused_computation.12 | convolution fusion | flops 1815740416 | bytes 9439492 | tf_op jit(solution)/shard_map/dot_general | solution.py:34
  149.3 75.9 %psum.7 = f32[]{:T(128)} all-reduce(f32[]{:T(128)} %get-tuple-element.20), channel_id=1, replica_groups=mesh['rep'=8,'fsdp'=32] {'fsdp'}, use_global_device_ids=true, to_apply=%region_6.7 | all-reduce | flops 1 | bytes 8 | tf_op jit(solution)/shard_map/psum | solution.py:62
  225.9 2.5 multiply_convert_fusion
  228.4 2.4 convert_element_type.23
  230.8 8.7 %reshape.135 = f32[9216,128]{1,0:T(8,128)} reshape(f32[96,192,64]{2,1,0:T(8,128)} %get-tuple-element.7) | data formatting | bytes 9437184 | tf_op jit(solution)/shard_map/add | solution.py:27
  239.5 7.7 %fusion.1 = f32[9216,128]{1,0:T(8,128)} fusion(f32[9216,128]{1,0:T(8,128)} %reshape.135, s32[128]{0:T(128)S(1)} %get-tuple-element.25, s32[128]{0:T(128)S(1)} %get-tuple-element.26, s32[128]{0:T(128)S(1)} %get-tuple-element.24, s32[128]{0:T(128)S(1)} %get-tuple-element.27, pred[128]{0:T(512)(128)(4,1)S(1)} %get-tuple-element.22, ...), kind=kOutput, calls=%fused_computation.34 | convolution fusion | flops 1812201472 | bytes 9439488 | tf_op jit(solution)/shard_map/dot_general | solution.py:34
  247.2 5.3 %reshape.134 = f32[1,96,12288]{2,1,0:T(8,128)} reshape(f32[9216,128]{1,0:T(8,128)} %fusion.1) | data formatting | bytes 9437184 | tf_op jit(solution)/shard_map/reshape | solution.py:36
  252.5 6.4 %sub.19 = f32[1,96,12288]{2,1,0:T(8,128)} subtract(f32[1,96,12288]{2,1,0:T(8,128)} %param.3, f32[1,96,12288]{2,1,0:T(8,128)} %reshape.134) | non-fusion elementwise | flops 1179648 | bytes 14155776 | tf_op jit(solution)/shard_map/sub | solution.py:58
  259.0 0.0 copy-done.1
  (10 shorter events, 0.2 us)
Async XLA Ops:
  7.2 30.2 %copy-start = (s32[8,96,192]{2,1,0:T(8,128)S(1)}, s32[8,96,192]{2,1,0:T(8,128)}, u32[]{:S(2)}) copy-start(s32[8,96,192]{2,1,0:T(8,128)} %param.5) | copy-start | bytes 1769476
  7.2 90.2 %all-gather.2.cloned.1.call-start = ((), (), s32[]{:S(2)}) async-start(), calls=%async_computation | async-start | bytes 3538944 | tf_op jit(solution)/shard_map/all_gather | solution.py:59
  247.2 11.8 %copy-start.1 = (s32[8,96,192]{2,1,0:T(8,128)S(1)}, s32[8,96,192]{2,1,0:T(8,128)}, u32[]{:S(2)}) copy-start(s32[8,96,192]{2,1,0:T(8,128)} %param.5) | copy-start | bytes 1769476
Sparse Core Ops, SparseCore 0:
  65.2 32.1 all-gather.1
where the time goes:
time: 267 us; the launch traced here: 266 us
  blocking collectives  75.9 us (28%)
  other arithmetic  71.4 us (27%)
  local copies, waits for them, and re-layouts  46.4 us (17%)
  waiting for transfers between devices  32.2 us (12%)
  matrix products  25 us (9%)
  between operations  14.8 us (6%)
    psum x1, blocking collectives, per_device(): energy = lax.psum(jnp.sum(raw * raw), 'fsdp')  75.9 us
    add x1, other arithmetic, to_dense(): dense + jnp.where(kept[..., slot:slot + 1] == freq_ids, values[..., slot:...  32.6 us
    all_gather x1, waiting for transfers between devices, per_device(): slot_vals = lax.all_gather(picked[None], 'rep', axis=0, tiled=True)  32.2 us
    reduce_sum x1, other arithmetic, per_device(): jnp.sum(jnp.where(kept[..., slot:slot + 1] == freq_ids, coeffs, 0.0), axi...  26.9 us
    add x2, local copies, waits for them, and re-layouts, to_dense(): dense + jnp.where(kept[..., slot:slot + 1] == freq_ids, values[..., slot:...  17.4 us
    dot_general x2, matrix products, decode(): jnp.dot(dense_part.reshape(-1, 2 * CH), basis_pair, precision=lax.Precisi...  16.1 us
    dot_general x1, matrix products, per_device(): jnp.dot(moment.reshape(-1, 2 * CH), basis_pair.T, precision=lax.Precision...  8.91 us
    reshape x1, local copies, waits for them, and re-layouts, per_device(): coeffs = jnp.dot(moment.reshape(-1, 2 * CH), basis_pair.T, precision=lax....  7.96 us
  transfers between devices with their start and end apart: 1, of which 1 were waited for; matrix products, arithmetic and copies ran while one was open for 0% of the time, Pallas kernels for 0%

commit v1 on v0

v1 whole, which is shorter than its diff:
```python
import functools
import math

import jax
import jax.numpy as jnp
import ml_dtypes
import numpy as np
from jax import lax
from jax.experimental import pallas as pl
from jax.experimental.pallas import tpu as pltpu
from jax.sharding import PartitionSpec as P

CH = 64
KEEP = 4
LANES = 128
PAIR = LANES // CH
CELLS = LANES // KEEP
TILES = CELLS // PAIR
WIDTH = TILES * LANES


def pair_table():
    k, n = np.arange(CH)[:, None], np.arange(CH)[None, :]
    basis = np.cos(math.pi * (2 * n + 1) * k / (2 * CH)) * math.sqrt(2 / CH)
    basis[0] = math.sqrt(1 / CH)
    return np.kron(np.eye(PAIR), basis)


def split_weights(table):
    high = table.astype(ml_dtypes.bfloat16)
    low = (table - high.astype(np.float64)).astype(ml_dtypes.bfloat16)
    side = np.concatenate([high, low], axis=1)
    return np.concatenate([side, side], axis=0)


def halves(x):
    high = x.astype(jnp.bfloat16)
    low = (x - high.astype(jnp.float32)).astype(jnp.bfloat16)
    return jnp.concatenate([high, low], axis=1)


def apply_table(tiles, weights):
    rows = tiles[0].shape[0]
    stacked = jnp.concatenate([halves(tile) for tile in tiles], axis=0)
    out = jnp.dot(stacked, weights, preferred_element_type=jnp.float32)
    out = out[:, :LANES] + out[:, LANES:]
    return [out[i * rows : (i + 1) * rows] for i in range(len(tiles))]


def lane_gather(x, index):
    return jnp.take_along_axis(x, index, axis=1, mode="promise_in_bounds")


def lane_ids(rows):
    return lax.broadcasted_iota(jnp.int32, (rows, LANES), 1)


def spread(ref_value, group, rows):
    start = group * CELLS
    base = start // LANES * LANES
    part = ref_value[:, base : base + LANES]
    if part.shape[1] < LANES:
        part = jnp.pad(part, ((0, 0), (0, LANES - part.shape[1])))
    return lane_gather(part, start - base + lane_ids(rows) % CELLS)


def pick_kernel(groups, rep_ref, x_ref, kept_ref, cnt_ref, w_ref, slot_ref, mine_ref, other_ref, scr):
    step = pl.program_id(0)
    rows = x_ref.shape[1]
    lanes = lane_ids(rows)
    slot = lanes // CELLS
    cell = lanes % CELLS

    @pl.when(step == 0)
    def _():
        counts = cnt_ref[0]
        numbers = [kept_ref[:, s, :] for s in range(KEEP)]
        for g in range(groups):
            chosen = spread(numbers[0], g, rows)
            for s in range(1, KEEP):
                chosen = jnp.where(slot == s, spread(numbers[s], g, rows), chosen)
            live = slot < spread(counts, g, rows)
            slot_ref[g] = chosen
            scr[g] = jnp.where(live, 1.0, 0.0)

    index = slot_ref[step] + (cell % PAIR) * CH
    picked = jnp.zeros((rows, LANES), jnp.float32)
    batch = 8
    for first in range(0, TILES, batch):
        tiles = [x_ref[0, :, t * LANES : (t + 1) * LANES] for t in range(first, first + batch)]
        for t, coeffs in enumerate(apply_table(tiles, w_ref[...]), first):
            picked = jnp.where(cell // PAIR == t, lane_gather(coeffs, index), picked)
    picked = jnp.where(scr[step] > 0.0, picked, 0.0)
    half = groups // 2
    core = rep_ref[0] % 2
    here = step // half == core

    @pl.when(here)
    def _():
        mine_ref[step % half] = picked

    @pl.when(jnp.logical_not(here))
    def _():
        other_ref[step % half] = picked


def group_values(rep_ref, mine_ref, other_ref, step, half):
    here = step // half == rep_ref[0] % 2
    place = step % half
    return jnp.where(here, mine_ref[place], other_ref[place])


def residue_kernel(groups, rep_ref, x_ref, slot_ref, mine_ref, other_ref, w_ref, out_ref, place_ref):
    step = pl.program_id(0)
    rows = x_ref.shape[1]
    lanes = lane_ids(rows)
    values = group_values(rep_ref, mine_ref, other_ref, step, groups // 2)
    numbers = slot_ref[step]
    batch = 8
    for first in range(0, TILES, batch):
        dense = []
        for t in range(first, first + batch):
            place = jnp.full((rows, LANES), -1, jnp.int32)
            for s in range(KEEP):
                source = s * CELLS + t * PAIR + lanes // CH
                place = jnp.where(lane_gather(numbers, source) == lanes % CH, source, place)
            place_ref[step, t] = place
            dense.append(jnp.where(place >= 0, lane_gather(values, place & (LANES - 1)), 0.0))
        for t, decoded in enumerate(apply_table(dense, w_ref[...]), first):
            part = slice(t * LANES, (t + 1) * LANES)
            out_ref[0, :, part] = x_ref[0, :, part] - decoded


def update_kernel(groups, entries, replicas, rep_ref, place_ref, mine_ref, other_ref, energy_ref, w_ref, out_ref):
    step = pl.program_id(0)
    energy = jnp.sum(energy_ref[:, 0, :], axis=0, keepdims=True)
    scale = lax.rsqrt(energy / entries + 1e-06) / replicas
    values = group_values(rep_ref, mine_ref, other_ref, step, groups // 2) * scale
    batch = 8
    for first in range(0, TILES, batch):
        dense = []
        for t in range(first, first + batch):
            place = place_ref[step, t]
            dense.append(jnp.where(place >= 0, lane_gather(values, place & (LANES - 1)), 0.0))
        for t, decoded in enumerate(apply_table(dense, w_ref[...]), first):
            out_ref[:, t * LANES : (t + 1) * LANES] = decoded.astype(jnp.bfloat16)


def per_device(momentum, kept, counts):
    _, rows, width = momentum.shape
    blocks = width // CH
    groups = width // WIDTH
    half = groups // 2
    replicas = lax.axis_size("rep")
    shards = lax.axis_size("fsdp")
    rep = lax.axis_index("rep").astype(jnp.int32).reshape(1)
    basis = pair_table()
    forward = jnp.asarray(split_weights(basis.T))
    inverse = jnp.asarray(split_weights(basis))
    slots = jnp.transpose(kept, (0, 2, 1))

    def whole(shape):
        return pl.BlockSpec(shape, lambda g, rep_ref: (0,) * len(shape))

    half_shape = (half, rows, LANES)
    half_out = jax.ShapeDtypeStruct(half_shape, jnp.float32)
    x_spec = pl.BlockSpec((1, rows, WIDTH), lambda g, rep_ref: (0, 0, g))
    w_spec = whole(forward.shape)
    numbers, mine, other = pl.pallas_call(
        functools.partial(pick_kernel, groups),
        grid_spec=pltpu.PrefetchScalarGridSpec(
            num_scalar_prefetch=1,
            grid=(groups,),
            in_specs=[
                x_spec,
                whole((rows, KEEP, blocks)),
                pl.BlockSpec((1, rows, blocks), lambda g, rep_ref: (rep_ref[0], 0, 0)),
                w_spec,
            ],
            out_specs=[whole((groups, rows, LANES)), whole(half_shape), whole(half_shape)],
            scratch_shapes=[pltpu.VMEM((groups, rows, LANES), jnp.float32)],
        ),
        out_shape=[jax.ShapeDtypeStruct((groups, rows, LANES), jnp.int32), half_out, half_out],
        compiler_params=pltpu.CompilerParams(vmem_limit_bytes=32 << 20),
        name="pick",
    )(rep, momentum, slots, counts, forward)

    swap = [(i, i ^ 1) for i in range(replicas)]
    flat = (half * rows, LANES)
    chip = mine.reshape(flat) + lax.ppermute(other.reshape(flat), "rep", swap)
    parts = [chip]
    for away in (4, 2, 6):
        ring = [(i, (i + away) % replicas) for i in range(replicas)]
        parts.append(lax.ppermute(chip, "rep", ring))
    total = (parts[0] + parts[1]) + (parts[2] + parts[3])
    total_other = lax.ppermute(total, "rep", swap)

    new_moment, place = pl.pallas_call(
        functools.partial(residue_kernel, groups),
        grid_spec=pltpu.PrefetchScalarGridSpec(
            num_scalar_prefetch=1,
            grid=(groups,),
            in_specs=[
                x_spec,
                whole((groups, rows, LANES)),
                whole(half_shape),
                whole(half_shape),
                w_spec,
            ],
            out_specs=[x_spec, whole((groups, TILES, rows, LANES))],
        ),
        out_shape=[
            jax.ShapeDtypeStruct(momentum.shape, jnp.float32),
            jax.ShapeDtypeStruct((groups, TILES, rows, LANES), jnp.int32),
        ],
        compiler_params=pltpu.CompilerParams(vmem_limit_bytes=32 << 20),
        name="residue",
    )(rep, momentum, numbers, mine, other, inverse)

    energy = jnp.sum(jnp.square(total / replicas)) + jnp.sum(jnp.square(total_other / replicas))
    energies = lax.all_to_all(
        jnp.full((shards, 1, LANES), energy, jnp.float32), "fsdp", 0, 0, tiled=True
    )
    update = pl.pallas_call(
        functools.partial(update_kernel, groups, rows * width * shards, replicas),
        grid_spec=pltpu.PrefetchScalarGridSpec(
            num_scalar_prefetch=1,
            grid=(groups,),
            in_specs=[
                whole((groups, TILES, rows, LANES)),
                whole(half_shape),
                whole(half_shape),
                whole((shards, 1, LANES)),
                w_spec,
            ],
            out_specs=pl.BlockSpec((rows, WIDTH), lambda g, rep_ref: (0, g)),
        ),
        out_shape=jax.ShapeDtypeStruct((rows, width), jnp.bfloat16),
        compiler_params=pltpu.CompilerParams(vmem_limit_bytes=32 << 20),
        name="update",
    )(rep, place, total.reshape(half_shape), total_other.reshape(half_shape), energies, inverse)
    return new_moment, update


def solution(mesh):
    placed = (P("rep", "fsdp", None), P("fsdp", None, None), P(None, "fsdp", None))
    return jax.shard_map(
        per_device,
        mesh=mesh,
        in_specs=placed,
        out_specs=(P("rep", "fsdp", None), P("fsdp", None)),
        check_vma=False,
    )
```

time: 267 us -> 72.2 us (0.27)
  the two profiles are of different devices: /device:TPU:8 before, /device:TPU:1 now
where the time goes in v1:
time: 72.2 us; the launch traced here: 71.8 us
  Pallas kernels  27.6 us (38%)
  starting transfers between devices  19.6 us (27%)
  local copies, waits for them, and re-layouts  12.8 us (18%)
  waiting for transfers between devices  8.46 us (12%)
  between operations  1.99 us (3%)
  other arithmetic  1.31 us (2%)
    pallas_call x1, Pallas kernels, per_device(): pl.pallas_call(functools.partial(residue_kernel, groups), grid_spec=pltpu...  17.4 us
    unnamed x16, local copies, waits for them, and re-layouts  12.2 us
    all_to_all x1, starting transfers between devices, per_device(): lax.all_to_all(jnp.full((shards, 1, LANES), energy, jnp.float32), 'fsdp',...  11 us
    ppermute x3, waiting for transfers between devices, per_device(): parts.append(lax.ppermute(chip, 'rep', ring))  6.44 us
    pallas_call x1, Pallas kernels, per_device(): pl.pallas_call(functools.partial(update_kernel, groups, rows * width * sh...  5.37 us
    pallas_call x1, Pallas kernels, per_device(): pl.pallas_call(functools.partial(pick_kernel, groups), grid_spec=pltpu.Pr...  4.91 us
    ppermute x1, starting transfers between devices, per_device(): chip = mine.reshape(flat) + lax.ppermute(other.reshape(flat), 'rep', swap)  3.33 us
    ppermute x3, starting transfers between devices, per_device(): parts.append(lax.ppermute(chip, 'rep', ring))  2.75 us
  transfers between devices with their start and end apart: 6, of which 5 were waited for; matrix products, arithmetic and copies ran while one was open for 0% of the time, Pallas kernels for 24%

profile of v1, /device:TPU:1, one launch (start us, length us, event | category | flops | bytes accessed | tf_op | source)
XLA Modules:
  0.0 71.8 jit_solution(9307892060525660014)
XLA Ops:
  0.6 2.3 %copy-done = f32[1,96,12288]{2,1,0:T(8,128)S(1)} copy-done((f32[1,96,12288]{2,1,0:T(8,128)S(1)}, f32[1,96,12288]{2,1,0:T(8,128)}, u32[]{:S(2)}) %copy-start) | copy-done | bytes 4718616
  3.0 1.1 %copy-done.4 = s32[8,96,192]{2,1,0:T(8,128)S(1)} copy-done((s32[8,96,192]{2,1,0:T(8,128)S(1)}, s32[8,96,192]{2,1,0:T(8,128)}, u32[]{:S(2)}) %copy-start.4) | copy-done | bytes 589848
  4.1 1.0 %copy-done.6 = s32[96,192,4]{1,2,0:T(4,128)S(1)} copy-done((s32[96,192,4]{1,2,0:T(4,128)S(1)}, s32[96,192,4]{1,2,0:T(4,128)}, u32[]{:S(2)}) %copy-start.6) | copy-done | bytes 294936
  5.1 0.9 %copy-done.7 = bf16[256,256]{1,0:T(8,128)(2,1)S(1)} copy-done((bf16[256,256]{1,0:T(8,128)(2,1)S(1)}, bf16[256,256]{1,0:T(8,128)(2,1)}, u32[]{:S(2)}) %copy-start.7) | copy-done | bytes 131096
  6.0 4.9 %pick.1 = (s32[6,96,128]{2,1,0:T(8,128)S(1)}, f32[3,96,128]{2,1,0:T(8,128)S(1)}, f32[3,96,128]{2,1,0:T(8,128)S(1)}) custom-call(s32[1]{0:T(128)} %bitcast.rep_ref, f32[1,96,12288]{2,1,0:T(8,128)S(1)} %copy-done, s32[96,4,192]{2,1,0:T(4,128)S(1)} %bitcast.9, s32[8,96,192]{2,1,0:T(8,128)S(1)} %copy-done.4, bf16[256,256]{1,0:T(8,128)(2,1)S(1)} %copy-done.7), custom_call_target="tpu_custom_call" | custom-call | tf_op jit(solution)/shard_map/pick/pallas_call | solution.py:169
  10.9 3.3 %collective-permute-start = (f32[288,128]{1,0:T(8,128)S(1)}, f32[288,128]{1,0:T(8,128)S(1)}, u32[]{:S(2)}, u32[]{:S(2)}) collective-permute-start(f32[288,128]{1,0:T(8,128)S(1)} %bitcast.10), channel_id=1, source_target_pairs={{0,32},{32,0},{64,96},{96,64},{128,160},{160,128},{192,224},{224,1... | collective-permute-start | bytes 442376 | tf_op jit(solution)/shard_map/ppermute | solution.py:190
  14.3 1.0 %collective-permute-done = f32[288,128]{1,0:T(8,128)S(1)} collective-permute-done((f32[288,128]{1,0:T(8,128)S(1)}, f32[288,128]{1,0:T(8,128)S(1)}, u32[]{:S(2)}, u32[]{:S(2)}) %collective-permute-start) | collective-permute-done | bytes 147488 | tf_op jit(solution)/shard_map/ppermute | solution.py:190
  15.3 1.1 %collective-permute-start.3 = (f32[288,128]{1,0:T(8,128)S(1)}, f32[288,128]{1,0:T(8,128)S(1)}, u32[]{:S(2)}, u32[]{:S(2)}) collective-permute-start(f32[288,128]{1,0:T(8,128)S(1)} %bitcast_add_fusion), channel_id=1, source_target_pairs={{0,192},{32,224},{64,0},{96,32},{128,64},{160,96},{192,128},{224,1... | collective-permute-start | bytes 442376 | tf_op jit(solution)/shard_map/ppermute | solution.py:194
  16.4 0.4 collective-permute-start.2
  16.8 1.2 %collective-permute-start.1 = (f32[288,128]{1,0:T(8,128)S(1)}, f32[288,128]{1,0:T(8,128)S(1)}, u32[]{:S(2)}, u32[]{:S(2)}) collective-permute-start(f32[288,128]{1,0:T(8,128)S(1)} %bitcast_add_fusion), channel_id=1, source_target_pairs={{0,128},{32,160},{64,192},{96,224},{128,0},{160,32},{192,64},{224,... | collective-permute-start | bytes 442376 | tf_op jit(solution)/shard_map/ppermute | solution.py:194
  18.0 2.4 %collective-permute-done.3 = f32[288,128]{1,0:T(8,128)S(1)} collective-permute-done((f32[288,128]{1,0:T(8,128)S(1)}, f32[288,128]{1,0:T(8,128)S(1)}, u32[]{:S(2)}, u32[]{:S(2)}) %collective-permute-start.3) | collective-permute-done | bytes 147488 | tf_op jit(solution)/shard_map/ppermute | solution.py:194
  20.4 3.0 %collective-permute-done.2 = f32[288,128]{1,0:T(8,128)S(1)} collective-permute-done((f32[288,128]{1,0:T(8,128)S(1)}, f32[288,128]{1,0:T(8,128)S(1)}, u32[]{:S(2)}, u32[]{:S(2)}) %collective-permute-start.2) | collective-permute-done | bytes 147488 | tf_op jit(solution)/shard_map/ppermute | solution.py:194
  23.5 1.0 %collective-permute-done.1 = f32[288,128]{1,0:T(8,128)S(1)} collective-permute-done((f32[288,128]{1,0:T(8,128)S(1)}, f32[288,128]{1,0:T(8,128)S(1)}, u32[]{:S(2)}, u32[]{:S(2)}) %collective-permute-start.1) | collective-permute-done | bytes 147488 | tf_op jit(solution)/shard_map/ppermute | solution.py:194
  24.5 0.7 multiply_reduce_fusion.1
  25.1 2.5 %collective-permute-start.4 = (f32[288,128]{1,0:T(8,128)S(1)}, f32[288,128]{1,0:T(8,128)S(1)}, u32[]{:S(2)}, u32[]{:S(2)}) collective-permute-start(f32[288,128]{1,0:T(8,128)S(1)} %get-tuple-element.13), channel_id=1, source_target_pairs={{0,32},{32,0},{64,96},{96,64},{128,160},{160,128},{192,224},{224,1... | collective-permute-start | bytes 442376 | tf_op jit(solution)/shard_map/ppermute | solution.py:196
  27.7 1.0 %collective-permute-done.4 = f32[288,128]{1,0:T(8,128)S(1)} collective-permute-done((f32[288,128]{1,0:T(8,128)S(1)}, f32[288,128]{1,0:T(8,128)S(1)}, u32[]{:S(2)}, u32[]{:S(2)}) %collective-permute-start.4) | collective-permute-done | bytes 147488 | tf_op jit(solution)/shard_map/ppermute | solution.py:196
  28.7 0.6 multiply_reduce_fusion
  30.6 0.6 broadcast_in_dim.3
  31.2 11.0 %all-to-all-start = ((f32[32,1,128]{2,1,0:T(1,128)}), f32[32,1,128]{2,1,0:T(1,128)S(1)}, u32[]{:S(2)}, u32[]{:S(2)}) async-start(f32[32,1,128]{2,1,0:T(1,128)} %broadcast_in_dim.3), calls=%async_computation | async-start | bytes 32768 | tf_op jit(solution)/shard_map/all_to_all | solution.py:221
  42.3 2.3 %copy-done.1 = f32[1,96,12288]{2,1,0:T(8,128)S(1)} copy-done((f32[1,96,12288]{2,1,0:T(8,128)S(1)}, f32[1,96,12288]{2,1,0:T(8,128)}, u32[]{:S(2)}) %copy-start.1) | copy-done | bytes 4718616
  44.6 17.4 %residue.1 = (f32[1,96,12288]{2,1,0:T(8,128)}, s32[6,16,96,128]{3,2,1,0:T(8,128)S(1)}) custom-call(s32[1]{0:T(128)} %bitcast.rep_ref, f32[1,96,12288]{2,1,0:T(8,128)S(1)} %copy-done.1, s32[6,96,128]{2,1,0:T(8,128)S(1)} %get-tuple-element.7.slot_ref, f32[3,96,128]{2,1,0:T(8,128)S(1)} %get-tuple-element.8.mine_ref, ...), custom_call_target="tpu_custom_call" | custom-call | tf_op jit(solution)/shard_map/residue/pallas_call | solution.py:198
  62.0 2.1 %copy-done.2 = s32[6,16,96,128]{3,2,1,0:T(8,128)} copy-done((s32[6,16,96,128]{3,2,1,0:T(8,128)}, s32[6,16,96,128]{3,2,1,0:T(8,128)S(1)}, u32[]{:S(2)}) %copy-start.2) | copy-done | bytes 4718616
  64.1 2.3 %copy-done.3 = s32[6,16,96,128]{3,2,1,0:T(8,128)S(1)} copy-done((s32[6,16,96,128]{3,2,1,0:T(8,128)S(1)}, s32[6,16,96,128]{3,2,1,0:T(8,128)}, u32[]{:S(2)}) %copy-start.3) | copy-done | bytes 4718616
  66.5 5.4 %update.1 = bf16[96,12288]{1,0:T(8,128)(2,1)} custom-call(s32[1]{0:T(128)} %bitcast.rep_ref, s32[6,16,96,128]{3,2,1,0:T(8,128)S(1)} %copy-done.3, f32[3,96,128]{2,1,0:T(8,128)S(1)} %bitcast.7, f32[3,96,128]{2,1,0:T(8,128)S(1)} %bitcast.8, f32[32,1,128]{2,1,0:T(1,128)S(1)} %all-to-all-done.energy_ref, bf16[256,256]{1,0:T(8,128)(2,1)S(1)} %copy-done.5), custom_call_target="tpu_custom_call" | custom-call | tf_op jit(solution)/shard_map/update/pallas_call | solution.py:224
  (11 shorter events, 0.0 us)
Async XLA Ops:
  0.6 2.3 %copy-start = (f32[1,96,12288]{2,1,0:T(8,128)S(1)}, f32[1,96,12288]{2,1,0:T(8,128)}, u32[]{:S(2)}) copy-start(f32[1,96,12288]{2,1,0:T(8,128)} %x_ref.3) | copy-start | bytes 14155780
  3.0 1.1 %copy-start.4 = (s32[8,96,192]{2,1,0:T(8,128)S(1)}, s32[8,96,192]{2,1,0:T(8,128)}, u32[]{:S(2)}) copy-start(s32[8,96,192]{2,1,0:T(8,128)} %cnt_ref.1) | copy-start | bytes 1769476
  4.1 1.0 %copy-start.6 = (s32[96,192,4]{1,2,0:T(4,128)S(1)}, s32[96,192,4]{1,2,0:T(4,128)}, u32[]{:S(2)}) copy-start(s32[96,192,4]{1,2,0:T(4,128)} %param.6) | copy-start | bytes 884740
  5.1 0.9 %copy-start.7 = (bf16[256,256]{1,0:T(8,128)(2,1)S(1)}, bf16[256,256]{1,0:T(8,128)(2,1)}, u32[]{:S(2)}) copy-start(bf16[256,256]{1,0:T(8,128)(2,1)} %constant.16.clone.w_ref) | copy-start | bytes 393220
  6.0 36.3 %copy-start.5 = (bf16[256,256]{1,0:T(8,128)(2,1)S(1)}, bf16[256,256]{1,0:T(8,128)(2,1)}, u32[]{:S(2)}) copy-start(bf16[256,256]{1,0:T(8,128)(2,1)} %constant.17.clone.w_ref) | copy-start | bytes 393220
  10.9 4.3 %collective-permute-start = (f32[288,128]{1,0:T(8,128)S(1)}, f32[288,128]{1,0:T(8,128)S(1)}, u32[]{:S(2)}, u32[]{:S(2)}) collective-permute-start(f32[288,128]{1,0:T(8,128)S(1)} %bitcast.10), channel_id=1, source_target_pairs={{0,32},{32,0},{64,96},{96,64},{128,160},{160,128},{192,224},{224,1... | collective-permute-start | bytes 442376 | tf_op jit(solution)/shard_map/ppermute | solution.py:190
  15.3 5.1 %collective-permute-start.3 = (f32[288,128]{1,0:T(8,128)S(1)}, f32[288,128]{1,0:T(8,128)S(1)}, u32[]{:S(2)}, u32[]{:S(2)}) collective-permute-start(f32[288,128]{1,0:T(8,128)S(1)} %bitcast_add_fusion), channel_id=1, source_target_pairs={{0,192},{32,224},{64,0},{96,32},{128,64},{160,96},{192,128},{224,1... | collective-permute-start | bytes 442376 | tf_op jit(solution)/shard_map/ppermute | solution.py:194
  16.4 7.1 %collective-permute-start.2 = (f32[288,128]{1,0:T(8,128)S(1)}, f32[288,128]{1,0:T(8,128)S(1)}, u32[]{:S(2)}, u32[]{:S(2)}) collective-permute-start(f32[288,128]{1,0:T(8,128)S(1)} %bitcast_add_fusion), channel_id=1, source_target_pairs={{0,64},{32,96},{64,128},{96,160},{128,192},{160,224},{192,0},{224,... | collective-permute-start | bytes 442376 | tf_op jit(solution)/shard_map/ppermute | solution.py:194
  16.8 7.6 %collective-permute-start.1 = (f32[288,128]{1,0:T(8,128)S(1)}, f32[288,128]{1,0:T(8,128)S(1)}, u32[]{:S(2)}, u32[]{:S(2)}) collective-permute-start(f32[288,128]{1,0:T(8,128)S(1)} %bitcast_add_fusion), channel_id=1, source_target_pairs={{0,128},{32,160},{64,192},{96,224},{128,0},{160,32},{192,64},{224,... | collective-permute-start | bytes 442376 | tf_op jit(solution)/shard_map/ppermute | solution.py:194
  25.1 3.6 %collective-permute-start.4 = (f32[288,128]{1,0:T(8,128)S(1)}, f32[288,128]{1,0:T(8,128)S(1)}, u32[]{:S(2)}, u32[]{:S(2)}) collective-permute-start(f32[288,128]{1,0:T(8,128)S(1)} %get-tuple-element.13), channel_id=1, source_target_pairs={{0,32},{32,0},{64,96},{96,64},{128,160},{160,128},{192,224},{224,1... | collective-permute-start | bytes 442376 | tf_op jit(solution)/shard_map/ppermute | solution.py:196
  31.2 32.9 %all-to-all-start = ((f32[32,1,128]{2,1,0:T(1,128)}), f32[32,1,128]{2,1,0:T(1,128)S(1)}, u32[]{:S(2)}, u32[]{:S(2)}) async-start(f32[32,1,128]{2,1,0:T(1,128)} %broadcast_in_dim.3), calls=%async_computation | async-start | bytes 32768 | tf_op jit(solution)/shard_map/all_to_all | solution.py:221
  42.3 2.3 %copy-start.1 = (f32[1,96,12288]{2,1,0:T(8,128)S(1)}, f32[1,96,12288]{2,1,0:T(8,128)}, u32[]{:S(2)}) copy-start(f32[1,96,12288]{2,1,0:T(8,128)} %x_ref.3) | copy-start | bytes 14155780
  62.0 2.1 %copy-start.2 = (s32[6,16,96,128]{3,2,1,0:T(8,128)}, s32[6,16,96,128]{3,2,1,0:T(8,128)S(1)}, u32[]{:S(2)}) copy-start(s32[6,16,96,128]{3,2,1,0:T(8,128)S(1)} %get-tuple-element.11.place_ref) | copy-start | bytes 14155780
  64.1 2.3 %copy-start.3 = (s32[6,16,96,128]{3,2,1,0:T(8,128)S(1)}, s32[6,16,96,128]{3,2,1,0:T(8,128)}, u32[]{:S(2)}) copy-start(s32[6,16,96,128]{3,2,1,0:T(8,128)} %copy-done.2) | copy-start | bytes 14155780

commit v2 on v0

v2 whole, which is shorter than its diff:
```python
import functools
import math

import jax
import jax.numpy as jnp
import ml_dtypes
import numpy as np
from jax import lax
from jax.experimental import pallas as pl
from jax.experimental.pallas import tpu as pltpu
from jax.sharding import PartitionSpec as P

CH = 64
KEEP = 4
LANES = 128
PACK = 16
PAIR = LANES // CH
CELLS = LANES // KEEP
TILES = CELLS // PAIR
WIDTH = TILES * LANES
BF = jnp.bfloat16
VMEM_BYTES = 32 << 20


def pair_table():
    k, n = np.arange(CH)[:, None], np.arange(CH)[None, :]
    basis = np.cos(math.pi * (2 * n + 1) * k / (2 * CH)) * math.sqrt(2 / CH)
    basis[0] = math.sqrt(1 / CH)
    return np.kron(np.eye(PAIR), basis)


def split_weights(table):
    high = table.astype(ml_dtypes.bfloat16)
    low = (table - high.astype(np.float64)).astype(ml_dtypes.bfloat16)
    side = np.concatenate([high, low], axis=1)
    return np.concatenate([side, side], axis=0)


def halves(x):
    high = x.astype(BF)
    return high, (x - high.astype(jnp.float32)).astype(BF)


def apply_weights(tiles, weights):
    rows = tiles[0].shape[0]
    out = jnp.dot(jnp.concatenate(tiles, axis=0), weights, preferred_element_type=jnp.float32)
    out = out[:, :LANES] + out[:, LANES:]
    return [out[i * rows : (i + 1) * rows] for i in range(len(tiles))]


def lane_gather(x, index):
    return jnp.take_along_axis(x, index, axis=1, mode="promise_in_bounds")


def lane_ids(rows):
    return lax.broadcasted_iota(jnp.int32, (rows, LANES), 1)


def spread(value, group, rows):
    start = group * CELLS
    base = start // LANES * LANES
    part = value[:, base : base + LANES]
    if part.shape[1] < LANES:
        part = jnp.pad(part, ((0, 0), (0, LANES - part.shape[1])))
    return lane_gather(part, start - base + lane_ids(rows) % CELLS)


def flip(x):
    fill = LANES - x.shape[0]
    return jnp.concatenate([x, x[:fill]], axis=0).T if fill else x.T


def columns(group):
    return pl.ds(pl.multiple_of(group * WIDTH, WIDTH), WIDTH)


def pick_kernel(
    rep_ref, x_hbm, kept_hbm, cnt_hbm, w_hbm, flip_ref, mine_ref, other_ref, x_ref,
    kept_ref, cnt_ref, w_ref, index_ref, live_ref, coeff_ref, small_sem, x_sem,
):
    groups, rows, _ = x_ref.shape
    half = groups // 2
    small = [
        pltpu.make_async_copy(kept_hbm, kept_ref, small_sem.at[0]),
        pltpu.make_async_copy(cnt_hbm.at[rep_ref[0]], cnt_ref, small_sem.at[1]),
        pltpu.make_async_copy(w_hbm, w_ref, small_sem.at[2]),
    ]
    for copy in small:
        copy.start()
    for g in range(groups):
        pltpu.make_async_copy(x_hbm.at[0, :, columns(g)], x_ref.at[g], x_sem.at[g]).start()
    for copy in small:
        copy.wait()

    lanes = lane_ids(rows)
    slot = lanes // CELLS
    counts = cnt_ref[...]
    numbers = [kept_ref[:, s, :] for s in range(KEEP)]
    for g in range(groups):
        chosen = spread(numbers[0], g, rows)
        for s in range(1, KEEP):
            chosen = jnp.where(slot == s, spread(numbers[s], g, rows), chosen)
        index_ref[g] = chosen + lanes % PAIR * CH
        flip_ref[g] = flip(chosen.astype(jnp.float32))
        live_ref[g] = jnp.where(slot < spread(counts, g, rows), 1.0, 0.0)

    tile_of = lane_ids(8) % CELLS // PAIR
    core = rep_ref[0] % 2

    def body(g, carry):
        pltpu.make_async_copy(x_hbm.at[0, :, columns(g)], x_ref.at[g], x_sem.at[g]).wait()
        tiles = [
            jnp.concatenate(halves(x_ref[g, :, t * LANES : (t + 1) * LANES]), axis=1)
            for t in range(TILES)
        ]
        for t, coeffs in enumerate(apply_weights(tiles, w_ref[...])):
            coeff_ref[t] = coeffs
        parts = []
        for first in range(0, rows, 8):
            here = slice(first, first + 8)
            index = index_ref[g, here]
            picked = jnp.zeros((8, LANES), jnp.float32)
            for t in range(TILES):
                picked = jnp.where(tile_of == t, lane_gather(coeff_ref[t, here], index), picked)
            parts.append(jnp.where(live_ref[g, here] > 0.0, picked, 0.0))
        picked = jnp.concatenate(parts, axis=0)

        @pl.when(g // half == core)
        def _():
            mine_ref[g % half] = picked

        @pl.when(g // half != core)
        def _():
            other_ref[g % half] = picked

        return carry

    lax.fori_loop(0, groups, body, 0)


def decode_group(flip_ref, g, values, w_ref, high_ref, low_ref):
    rows = values.shape[0]
    turned = flip(values)
    high = turned.astype(BF).astype(jnp.float32)
    high_ref[...] = high
    low_ref[...] = turned - high
    number = lax.broadcasted_iota(jnp.int32, (PACK, LANES), 0).astype(jnp.float32)
    zero = jnp.zeros((PACK, LANES), BF)

    def row(values_ref, s, cell):
        at = s * CELLS + cell
        return jnp.broadcast_to(values_ref[at : at + 1, :], (PACK, LANES)).astype(BF)

    tiles = []
    for t in range(TILES):
        highs, lows = [], []
        for cell in range(t * PAIR, (t + 1) * PAIR):
            kept = [row(flip_ref.at[g], s, cell) for s in range(KEEP)]
            cell_high = [row(high_ref, s, cell) for s in range(KEEP)]
            cell_low = [row(low_ref, s, cell) for s in range(KEEP)]
            for first in range(0, CH, PACK):
                ids = (number + first).astype(BF)
                dense_high, dense_low = zero, zero
                for s in range(KEEP):
                    hit = kept[s] == ids
                    dense_high = jnp.where(hit, cell_high[s], dense_high)
                    dense_low = jnp.where(hit, cell_low[s], dense_low)
                highs.append(dense_high)
                lows.append(dense_low)
        both = [jnp.concatenate(part, axis=0).T[:rows] for part in (highs, lows)]
        tiles.append(jnp.concatenate(both, axis=1))
    return apply_weights(tiles, w_ref[...])


def side(rep_ref, mine_ref, other_ref, g):
    half = mine_ref.shape[0]
    return jnp.where(g // half == rep_ref[0] % 2, mine_ref[g % half], other_ref[g % half])


def residue_kernel(
    rep_ref, x_ref, flip_ref, mine_ref, other_ref, w_ref, after_ref, out_hbm, done_ref,
    high_ref, low_ref, out_ref, sem,
):
    groups = x_ref.shape[0]
    done_ref[...] = jnp.zeros(done_ref.shape, jnp.float32)

    def copy(g):
        return pltpu.make_async_copy(out_ref.at[g], out_hbm.at[0, :, columns(g)], sem.at[g])

    def body(g, carry):
        values = side(rep_ref, mine_ref, other_ref, g)
        for t, part in enumerate(decode_group(flip_ref, g, values, w_ref, high_ref, low_ref)):
            here = slice(t * LANES, (t + 1) * LANES)
            out_ref[g, :, here] = x_ref[g, :, here] - part
        copy(g).start()
        return carry

    lax.fori_loop(0, groups, body, 0)
    for g in range(groups):
        copy(g).wait()


def total_kernel(a_ref, b_ref, c_ref, d_ref, after_ref, out_ref):
    out_ref[...] = (a_ref[...] + b_ref[...]) + (c_ref[...] + d_ref[...])


def energy_kernel(replicas, a_ref, b_ref, out_ref):
    square = jnp.square(a_ref[...] / replicas) + jnp.square(b_ref[...] / replicas)
    energy = jnp.sum(jnp.sum(square, axis=0, keepdims=True), axis=1, keepdims=True)
    out_ref[...] = jnp.broadcast_to(energy[None], out_ref.shape)


def update_kernel(
    entries, replicas, rep_ref, flip_ref, mine_ref, other_ref, energy_ref, w_ref, out_hbm,
    high_ref, low_ref, out_ref, sem,
):
    groups = out_ref.shape[0]
    energy = jnp.sum(energy_ref[:, 0, :], axis=0, keepdims=True)
    scale = lax.rsqrt(energy / entries + 1e-06) / replicas

    def copy(g):
        return pltpu.make_async_copy(out_ref.at[g], out_hbm.at[:, columns(g)], sem.at[g])

    def body(g, carry):
        values = side(rep_ref, mine_ref, other_ref, g) * scale
        for t, part in enumerate(decode_group(flip_ref, g, values, w_ref, high_ref, low_ref)):
            out_ref[g, :, t * LANES : (t + 1) * LANES] = part.astype(BF)
        copy(g).start()
        return carry

    lax.fori_loop(0, groups, body, 0)
    for g in range(groups):
        copy(g).wait()


def call(kernel, name, operands, out_shape, scratch=(), microseconds=1.0):
    specs, arrays = [], []
    for place, array in operands:
        specs.append(pl.BlockSpec(memory_space=place))
        arrays.append(pltpu.with_memory_space_constraint(array, place) if place is pltpu.HBM else array)
    shapes = out_shape if isinstance(out_shape, list) else [out_shape]
    outs = [
        pl.BlockSpec(memory_space=pltpu.HBM if shape.memory_space is pltpu.HBM else pltpu.VMEM)
        for shape in shapes
    ]
    return pl.pallas_call(
        kernel,
        in_specs=specs,
        out_specs=outs if isinstance(out_shape, list) else outs[0],
        out_shape=out_shape,
        scratch_shapes=list(scratch),
        compiler_params=pltpu.CompilerParams(vmem_limit_bytes=VMEM_BYTES),
        cost_estimate=pl.CostEstimate(
            flops=0, bytes_accessed=int(microseconds * 3.0e6), transcendentals=0
        ),
        name=name,
    )(*arrays)


def per_device(momentum, kept, counts):
    _, rows, width = momentum.shape
    blocks = width // CH
    groups = width // WIDTH
    half = groups // 2
    replicas = lax.axis_size("rep")
    shards = lax.axis_size("fsdp")
    rep = lax.axis_index("rep").astype(jnp.int32).reshape(1)
    basis = pair_table()
    forward = jnp.asarray(split_weights(basis.T))
    inverse = jnp.asarray(split_weights(basis))
    hbm, vmem, smem = pltpu.HBM, pltpu.VMEM, pltpu.SMEM
    half_shape = (half, rows, LANES)
    flat = (half * rows, LANES)
    dma = pltpu.SemaphoreType.DMA
    turned = [vmem((LANES, LANES), jnp.float32)] * 2

    flipped, mine, other, x = call(
        pick_kernel,
        "pick",
        [
            (smem, rep),
            (hbm, momentum),
            (hbm, jnp.transpose(kept, (0, 2, 1))),
            (hbm, counts),
            (hbm, forward),
        ],
        [
            vmem((groups, LANES, LANES), jnp.float32),
            vmem(half_shape, jnp.float32),
            vmem(half_shape, jnp.float32),
            vmem((groups, rows, WIDTH), jnp.float32),
        ],
        [
            vmem((rows, KEEP, blocks), jnp.int32),
            vmem((rows, blocks), jnp.int32),
            vmem(forward.shape, BF),
            vmem((groups, rows, LANES), jnp.int32),
            vmem((groups, rows, LANES), jnp.float32),
            vmem((TILES, rows, LANES), jnp.float32),
            dma((3,)),
            dma((groups,)),
        ],
        5.0,
    )

    swap = [(i, i ^ 1) for i in range(replicas)]
    chip = mine.reshape(flat) + lax.ppermute(other.reshape(flat), "rep", swap)
    away = []
    for step in (4, 2, 6):
        ring = [(i, (i + step) % replicas) for i in range(replicas)]
        away.append(lax.ppermute(chip, "rep", ring))

    new_moment, done = call(
        residue_kernel,
        "residue",
        [(smem, rep), (vmem, x), (vmem, flipped), (vmem, mine), (vmem, other), (vmem, inverse), (vmem, chip)],
        [hbm(momentum.shape, jnp.float32), vmem((8, LANES), jnp.float32)],
        turned + [vmem((groups, rows, WIDTH), jnp.float32), dma((groups,))],
        5.0,
    )
    total = call(
        total_kernel,
        "total",
        [(vmem, chip)] + [(vmem, part) for part in away] + [(vmem, done)],
        vmem(flat, jnp.float32),
        microseconds=0.5,
    )
    total_other = lax.ppermute(total, "rep", swap)
    energies = call(
        functools.partial(energy_kernel, replicas),
        "energy",
        [(vmem, total), (vmem, total_other)],
        vmem((shards, 1, LANES), jnp.float32),
        microseconds=0.5,
    )
    energies = lax.all_to_all(energies, "fsdp", 0, 0, tiled=True)
    update = call(
        functools.partial(update_kernel, rows * width * shards, replicas),
        "update",
        [
            (smem, rep),
            (vmem, flipped),
            (vmem, total.reshape(half_shape)),
            (vmem, total_other.reshape(half_shape)),
            (vmem, energies),
            (vmem, inverse),
        ],
        hbm((rows, width), BF),
        turned + [vmem((groups, rows, WIDTH), BF), dma((groups,))],
        4.0,
    )
    return new_moment, update


def solution(mesh):
    placed = (P("rep", "fsdp", None), P("fsdp", None, None), P(None, "fsdp", None))
    return jax.shard_map(
        per_device,
        mesh=mesh,
        in_specs=placed,
        out_specs=(P("rep", "fsdp", None), P("fsdp", None)),
        check_vma=False,
    )
```

time: 267 us -> 49 us (0.18)
  the two profiles are of different devices: /device:TPU:8 before, /device:TPU:1 now
where the time goes in v2:
time: 49 us; the launch traced here: 48.9 us
  blocking collectives  19.4 us (40%)
  Pallas kernels  16.5 us (34%)
  starting transfers between devices  8.71 us (18%)
  waiting for transfers between devices  3.62 us (7%)
  between operations  0.68 us (1%)
    all_to_all x1, blocking collectives, per_device(): energies = lax.all_to_all(energies, 'fsdp', 0, 0, tiled=True)  19.4 us
    pallas_call x5, Pallas kernels, call(): pl.pallas_call(kernel, in_specs=specs, out_specs=outs if isinstance(out_s...  16.5 us
    ppermute x1, starting transfers between devices, per_device(): chip = mine.reshape(flat) + lax.ppermute(other.reshape(flat), 'rep', swap)  3.37 us
    ppermute x3, starting transfers between devices, per_device(): away.append(lax.ppermute(chip, 'rep', ring))  2.7 us
    ppermute x1, starting transfers between devices, per_device(): total_other = lax.ppermute(total, 'rep', swap)  2.64 us
    ppermute x3, waiting for transfers between devices, per_device(): away.append(lax.ppermute(chip, 'rep', ring))  1.61 us
    ppermute x1, waiting for transfers between devices, per_device(): chip = mine.reshape(flat) + lax.ppermute(other.reshape(flat), 'rep', swap)  1.01 us
    ppermute x1, waiting for transfers between devices, per_device(): total_other = lax.ppermute(total, 'rep', swap)  1.01 us
  transfers between devices with their start and end apart: 5, of which 4 were waited for; matrix products, arithmetic and copies ran while one was open for 0% of the time, Pallas kernels for 10%

profile of v2, /device:TPU:1, one launch (start us, length us, event | category | flops | bytes accessed | tf_op | source)
XLA Modules:
  0.0 48.9 jit_solution(2904886666059404485)
XLA Ops:
  0.6 0.0 copy-start
  0.6 6.8 %pick.1 = (f32[6,128,128]{2,1,0:T(8,128)S(1)}, f32[3,96,128]{2,1,0:T(8,128)S(1)}, f32[3,96,128]{2,1,0:T(8,128)S(1)}, f32[6,96,2048]{2,1,0:T(8,128)S(1)}) custom-call(s32[1]{0:T(128)} %bitcast.rep_ref, f32[1,96,12288]{2,1,0:T(8,128)} %x_hbm.1, s32[96,4,192]{2,1,0:T(4,128)} %bitcast.10, s32[8,96,192]{2,1,0:T(8,128)} %cnt_hbm.1, ...), custom_call_target="tpu_custom_call" | custom-call | bytes 15000000 | tf_op jit(solution)/shard_map/pick/pallas_call | solution.py:246
  7.4 3.4 %collective-permute-start = (f32[288,128]{1,0:T(8,128)S(1)}, f32[288,128]{1,0:T(8,128)S(1)}, u32[]{:S(2)}, u32[]{:S(2)}) collective-permute-start(f32[288,128]{1,0:T(8,128)S(1)} %bitcast.9), channel_id=1, source_target_pairs={{0,32},{32,0},{64,96},{96,64},{128,160},{160,128},{192,224},{224,1... | collective-permute-start | bytes 442376 | tf_op jit(solution)/shard_map/ppermute | solution.py:307
  10.8 1.0 %collective-permute-done = f32[288,128]{1,0:T(8,128)S(1)} collective-permute-done((f32[288,128]{1,0:T(8,128)S(1)}, f32[288,128]{1,0:T(8,128)S(1)}, u32[]{:S(2)}, u32[]{:S(2)}) %collective-permute-start) | collective-permute-done | bytes 147488 | tf_op jit(solution)/shard_map/ppermute | solution.py:307
  11.8 1.1 %collective-permute-start.3 = (f32[288,128]{1,0:T(8,128)S(1)}, f32[288,128]{1,0:T(8,128)S(1)}, u32[]{:S(2)}, u32[]{:S(2)}) collective-permute-start(f32[288,128]{1,0:T(8,128)S(1)} %bitcast_add_fusion.after_ref.a_ref), channel_id=1, source_target_pairs={{0,192},{32,224},{64,0},{96,32},{128,64},{160,96},{192,128},{224,1... | collective-permute-start | bytes 442376 | tf_op jit(solution)/shard_map/ppermute | solution.py:311
  12.9 0.5 collective-permute-start.2
  13.4 1.2 %collective-permute-start.1 = (f32[288,128]{1,0:T(8,128)S(1)}, f32[288,128]{1,0:T(8,128)S(1)}, u32[]{:S(2)}, u32[]{:S(2)}) collective-permute-start(f32[288,128]{1,0:T(8,128)S(1)} %bitcast_add_fusion.after_ref.a_ref), channel_id=1, source_target_pairs={{0,128},{32,160},{64,192},{96,224},{128,0},{160,32},{192,64},{224,... | collective-permute-start | bytes 442376 | tf_op jit(solution)/shard_map/ppermute | solution.py:311
  14.6 0.0 copy-done
  14.6 4.8 %residue.1 = (f32[1,96,12288]{2,1,0:T(8,128)}, f32[8,128]{1,0:T(8,128)S(1)}) custom-call(s32[1]{0:T(128)} %bitcast.rep_ref, f32[6,96,2048]{2,1,0:T(8,128)S(1)} %get-tuple-element.8.x_ref, f32[6,128,128]{2,1,0:T(8,128)S(1)} %get-tuple-element.9.flip_ref, f32[3,96,128]{2,1,0:T(8,128)S(1)} %get-tuple-element.10.mine_ref, ...), custom_call_target="tpu_custom_call" | custom-call | bytes 15000000 | tf_op jit(solution)/shard_map/residue/pallas_call | solution.py:246
  19.4 0.0 collective-permute-done.3.d_ref
  19.4 0.6 %collective-permute-done.2.c_ref = f32[288,128]{1,0:T(8,128)S(1)} collective-permute-done((f32[288,128]{1,0:T(8,128)S(1)}, f32[288,128]{1,0:T(8,128)S(1)}, u32[]{:S(2)}, u32[]{:S(2)}) %collective-permute-start.2) | collective-permute-done | bytes 147488 | tf_op jit(solution)/shard_map/ppermute | solution.py:311
  20.0 1.0 %collective-permute-done.1.b_ref = f32[288,128]{1,0:T(8,128)S(1)} collective-permute-done((f32[288,128]{1,0:T(8,128)S(1)}, f32[288,128]{1,0:T(8,128)S(1)}, u32[]{:S(2)}, u32[]{:S(2)}) %collective-permute-start.1) | collective-permute-done | bytes 147488 | tf_op jit(solution)/shard_map/ppermute | solution.py:311
  21.0 2.6 %collective-permute-start.4 = (f32[288,128]{1,0:T(8,128)S(1)}, f32[288,128]{1,0:T(8,128)S(1)}, u32[]{:S(2)}, u32[]{:S(2)}) collective-permute-start(f32[288,128]{1,0:T(8,128)S(1)} %total.1.a_ref), channel_id=1, source_target_pairs={{0,32},{32,0},{64,96},{96,64},{128,160},{160,128},{192,224},{224,1... | collective-permute-start | bytes 442376 | tf_op jit(solution)/shard_map/ppermute | solution.py:328
  23.7 1.0 %collective-permute-done.4.b_ref = f32[288,128]{1,0:T(8,128)S(1)} collective-permute-done((f32[288,128]{1,0:T(8,128)S(1)}, f32[288,128]{1,0:T(8,128)S(1)}, u32[]{:S(2)}, u32[]{:S(2)}) %collective-permute-start.4) | collective-permute-done | bytes 147488 | tf_op jit(solution)/shard_map/ppermute | solution.py:328
  24.7 0.1 energy.1
  24.8 19.4 %all_to_all.5.energy_ref = f32[32,1,128]{2,1,0:T(1,128)S(1)} all-to-all(f32[32,1,128]{2,1,0:T(1,128)S(1)} %energy.1), channel_id=1, replica_groups=mesh['rep'=8,'fsdp'=32] {'fsdp'}, dimensions={0} | all-to-all | bytes 32768 | tf_op jit(solution)/shard_map/all_to_all | solution.py:336
  44.2 4.7 %update.1 = bf16[96,12288]{1,0:T(8,128)(2,1)} custom-call(s32[1]{0:T(128)} %bitcast.rep_ref, f32[6,128,128]{2,1,0:T(8,128)S(1)} %get-tuple-element.9.flip_ref, f32[3,96,128]{2,1,0:T(8,128)S(1)} %bitcast.7, f32[3,96,128]{2,1,0:T(8,128)S(1)} %bitcast.8, f32[32,1,128]{2,1,0:T(1,128)S(1)} %all_to_all.5.energy_ref, bf16[256,256]{1,0:T(8,128)(2,1)S(1)} %copy-done), custom_call_target="tpu_custom_call" | custom-call | bytes 12000000 | tf_op jit(solution)/shard_map/update/pallas_call | solution.py:246
  (2 shorter events, 0.1 us)
Async XLA Ops:
  0.6 13.9 %copy-start = (bf16[256,256]{1,0:T(8,128)(2,1)S(1)}, bf16[256,256]{1,0:T(8,128)(2,1)}, u32[]{:S(2)}) copy-start(bf16[256,256]{1,0:T(8,128)(2,1)} %constant.11.clone.w_ref) | copy-start | bytes 393220
  7.4 4.4 %collective-permute-start = (f32[288,128]{1,0:T(8,128)S(1)}, f32[288,128]{1,0:T(8,128)S(1)}, u32[]{:S(2)}, u32[]{:S(2)}) collective-permute-start(f32[288,128]{1,0:T(8,128)S(1)} %bitcast.9), channel_id=1, source_target_pairs={{0,32},{32,0},{64,96},{96,64},{128,160},{160,128},{192,224},{224,1... | collective-permute-start | bytes 442376 | tf_op jit(solution)/shard_map/ppermute | solution.py:307
  11.8 7.5 %collective-permute-start.3 = (f32[288,128]{1,0:T(8,128)S(1)}, f32[288,128]{1,0:T(8,128)S(1)}, u32[]{:S(2)}, u32[]{:S(2)}) collective-permute-start(f32[288,128]{1,0:T(8,128)S(1)} %bitcast_add_fusion.after_ref.a_ref), channel_id=1, source_target_pairs={{0,192},{32,224},{64,0},{96,32},{128,64},{160,96},{192,128},{224,1... | collective-permute-start | bytes 442376 | tf_op jit(solution)/shard_map/ppermute | solution.py:311
  12.9 7.1 %collective-permute-start.2 = (f32[288,128]{1,0:T(8,128)S(1)}, f32[288,128]{1,0:T(8,128)S(1)}, u32[]{:S(2)}, u32[]{:S(2)}) collective-permute-start(f32[288,128]{1,0:T(8,128)S(1)} %bitcast_add_fusion.after_ref.a_ref), channel_id=1, source_target_pairs={{0,64},{32,96},{64,128},{96,160},{128,192},{160,224},{192,0},{224,... | collective-permute-start | bytes 442376 | tf_op jit(solution)/shard_map/ppermute | solution.py:311
  13.4 7.6 %collective-permute-start.1 = (f32[288,128]{1,0:T(8,128)S(1)}, f32[288,128]{1,0:T(8,128)S(1)}, u32[]{:S(2)}, u32[]{:S(2)}) collective-permute-start(f32[288,128]{1,0:T(8,128)S(1)} %bitcast_add_fusion.after_ref.a_ref), channel_id=1, source_target_pairs={{0,128},{32,160},{64,192},{96,224},{128,0},{160,32},{192,64},{224,... | collective-permute-start | bytes 442376 | tf_op jit(solution)/shard_map/ppermute | solution.py:311
  21.0 3.6 %collective-permute-start.4 = (f32[288,128]{1,0:T(8,128)S(1)}, f32[288,128]{1,0:T(8,128)S(1)}, u32[]{:S(2)}, u32[]{:S(2)}) collective-permute-start(f32[288,128]{1,0:T(8,128)S(1)} %total.1.a_ref), channel_id=1, source_target_pairs={{0,32},{32,0},{64,96},{96,64},{128,160},{160,128},{192,224},{224,1... | collective-permute-start | bytes 442376 | tf_op jit(solution)/shard_map/ppermute | solution.py:328

commit v3 on v2

v3 whole, which is shorter than its diff:
```python
import functools
import math

import jax
import jax.numpy as jnp
import ml_dtypes
import numpy as np
from jax import lax
from jax.experimental import pallas as pl
from jax.experimental.pallas import tpu as pltpu
from jax.sharding import PartitionSpec as P

CH = 64
KEEP = 4
LANES = 128
PACK = 16
PAIR = LANES // CH
CELLS = LANES // KEEP
TILES = CELLS // PAIR
WIDTH = TILES * LANES
BF = jnp.bfloat16
VMEM_BYTES = 32 << 20
CHUNKS = 4


def pair_table():
    k, n = np.arange(CH)[:, None], np.arange(CH)[None, :]
    basis = np.cos(math.pi * (2 * n + 1) * k / (2 * CH)) * math.sqrt(2 / CH)
    basis[0] = math.sqrt(1 / CH)
    return np.kron(np.eye(PAIR), basis)


def split_weights(table):
    high = table.astype(ml_dtypes.bfloat16)
    low = (table - high.astype(np.float64)).astype(ml_dtypes.bfloat16)
    side = np.concatenate([high, low], axis=1)
    return np.concatenate([side, side], axis=0)


def halves(x):
    high = x.astype(BF)
    return high, (x - high.astype(jnp.float32)).astype(BF)


def apply_weights(tiles, weights):
    rows = tiles[0].shape[0]
    out = jnp.dot(jnp.concatenate(tiles, axis=0), weights, preferred_element_type=jnp.float32)
    out = out[:, :LANES] + out[:, LANES:]
    return [out[i * rows : (i + 1) * rows] for i in range(len(tiles))]


def lane_gather(x, index):
    return jnp.take_along_axis(x, index, axis=1, mode="promise_in_bounds")


def lane_ids(rows):
    return lax.broadcasted_iota(jnp.int32, (rows, LANES), 1)


def spread(value, group, rows):
    start = group * CELLS
    base = start // LANES * LANES
    part = value[:, base : base + LANES]
    if part.shape[1] < LANES:
        part = jnp.pad(part, ((0, 0), (0, LANES - part.shape[1])))
    return lane_gather(part, start - base + lane_ids(rows) % CELLS)


def flip(x):
    fill = LANES - x.shape[0]
    return jnp.concatenate([x, x[:fill]], axis=0).T if fill else x.T


def columns(group):
    return pl.ds(pl.multiple_of(group * WIDTH, WIDTH), WIDTH)


def pick_kernel(
    rep_ref, x_hbm, kept_hbm, cnt_hbm, w_hbm, number_ref, mine_ref, other_ref, x_ref,
    kept_ref, cnt_ref, w_ref, live_ref, coeff_ref, small_sem, x_sem,
):
    groups, rows, _ = x_ref.shape
    half = groups // 2
    small = [
        pltpu.make_async_copy(w_hbm, w_ref, small_sem.at[0]),
        pltpu.make_async_copy(kept_hbm, kept_ref, small_sem.at[1]),
        pltpu.make_async_copy(cnt_hbm.at[rep_ref[0]], cnt_ref, small_sem.at[2]),
    ]
    for copy in small:
        copy.start()

    def x_copy(g):
        return pltpu.make_async_copy(x_hbm.at[0, :, columns(g)], x_ref.at[g], x_sem.at[g])

    for g in range(groups):
        x_copy(g).start()
    for copy in small:
        copy.wait()

    slot = lane_ids(rows) // CELLS
    counts = cnt_ref[...]
    numbers = [kept_ref[:, s, :] for s in range(KEEP)]
    for g in range(groups):
        chosen = spread(numbers[0], g, rows)
        for s in range(1, KEEP):
            chosen = jnp.where(slot == s, spread(numbers[s], g, rows), chosen)
        number_ref[g] = chosen
        live_ref[g] = jnp.where(slot < spread(counts, g, rows), 1.0, 0.0)

    lanes = lane_ids(8)
    block_start = lanes % PAIR * CH
    tile_of = lanes % CELLS // PAIR
    core = rep_ref[0] % 2

    def transform(g, buffer, tiles):
        parts = [
            jnp.concatenate(halves(x_ref[g, :, t * LANES : (t + 1) * LANES]), axis=1) for t in tiles
        ]
        for t, coeffs in zip(tiles, apply_weights(parts, w_ref[...])):
            coeff_ref[buffer, t] = coeffs

    def choose(g, buffer, first):
        here = slice(first, first + 8)
        index = number_ref[g, here] + block_start
        picked = jnp.zeros((8, LANES), jnp.float32)
        for t in range(TILES):
            picked = jnp.where(tile_of == t, lane_gather(coeff_ref[buffer, t, here], index), picked)
        return jnp.where(live_ref[g, here] > 0.0, picked, 0.0)

    def put(g, parts):
        picked = jnp.concatenate(parts, axis=0)

        @pl.when(g // half == core)
        def _():
            mine_ref[g % half] = picked

        @pl.when(g // half != core)
        def _():
            other_ref[g % half] = picked

    def step(g, buffer):
        x_copy(g + 1).wait()
        parts = []
        for j in range(CHUNKS):
            transform(g + 1, 1 - buffer, span(TILES, j))
            parts += [choose(g, buffer, 8 * i) for i in span(rows // 8, j)]
        put(g, parts)

    x_copy(0).wait()
    transform(0, 0, range(TILES))
    two_by_two(step, groups - 1)
    last = groups - 1
    put(last, [choose(last, last % 2, first) for first in range(0, rows, 8)])


def span(count, j):
    return range(count * j // CHUNKS, count * (j + 1) // CHUNKS)


def two_by_two(step, count):
    def body(i, carry):
        step(2 * i, 0)
        step(2 * i + 1, 1)
        return carry

    lax.fori_loop(0, count // 2, body, 0)
    if count % 2:
        step(count - 1, (count - 1) % 2)


def decode(groups, numbers_of, values_of, w_ref, number_ref, high_ref, low_ref, dense_ref, store, unroll):
    rows = dense_ref.shape[1] // TILES
    ids = lax.broadcasted_iota(jnp.int32, (PACK, LANES), 0).astype(jnp.float32)
    ids = [(ids + first).astype(BF) for first in range(0, CH, PACK)]
    zero = jnp.zeros((PACK, LANES), BF)

    def turn(g, buffer):
        number_ref[buffer] = numbers_of(g)
        values = flip(values_of(g))
        high = values.astype(BF).astype(jnp.float32)
        high_ref[buffer] = high
        low_ref[buffer] = values - high

    def row(ref, buffer, s, cell):
        at = s * CELLS + cell
        return jnp.broadcast_to(ref[buffer, at : at + 1, :], (PACK, LANES)).astype(BF)

    def fill(buffer, tiles):
        for t in tiles:
            highs, lows = [], []
            for cell in range(t * PAIR, (t + 1) * PAIR):
                kept = [row(number_ref, buffer, s, cell) for s in range(KEEP)]
                cell_high = [row(high_ref, buffer, s, cell) for s in range(KEEP)]
                cell_low = [row(low_ref, buffer, s, cell) for s in range(KEEP)]
                for some in ids:
                    dense_high, dense_low = zero, zero
                    for s in range(KEEP):
                        hit = kept[s] == some
                        dense_high = jnp.where(hit, cell_high[s], dense_high)
                        dense_low = jnp.where(hit, cell_low[s], dense_low)
                    highs.append(dense_high)
                    lows.append(dense_low)
            here = slice(t * rows, (t + 1) * rows)
            dense_ref[buffer, here, :LANES] = jnp.concatenate(highs, axis=0).T[:rows]
            dense_ref[buffer, here, LANES:] = jnp.concatenate(lows, axis=0).T[:rows]

    def product(g, buffer, tiles):
        parts = [dense_ref[buffer, t * rows : (t + 1) * rows] for t in tiles]
        for t, part in zip(tiles, apply_weights(parts, w_ref[...])):
            store(g, t, part)

    def step(g, buffer):
        turn(g + 1, 1 - buffer)
        for j in range(CHUNKS):
            product(g, buffer, span(TILES, j))
            fill(1 - buffer, span(TILES, j))
        store(g, None, None)

    turn(0, 0)
    fill(0, range(TILES))
    if unroll:
        for g in range(groups - 1):
            step(g, g % 2)
    else:
        two_by_two(step, groups - 1)
    product(groups - 1, (groups - 1) % 2, range(TILES))
    store(groups - 1, None, None)


def side(rep_ref, mine_ref, other_ref, g):
    half = mine_ref.shape[0]
    return jnp.where(g // half == rep_ref[0] % 2, mine_ref[g % half], other_ref[g % half])


def residue_kernel(
    rep_ref, x_ref, chosen_ref, mine_ref, other_ref, w_ref, after_ref, out_hbm, flip_ref,
    number_ref, high_ref, low_ref, dense_ref, out_ref, sem,
):
    groups = x_ref.shape[0]

    def copy(g):
        return pltpu.make_async_copy(out_ref.at[g], out_hbm.at[0, :, columns(g)], sem.at[g])

    def numbers_of(g):
        turned = flip(chosen_ref[g].astype(jnp.float32))
        flip_ref[g] = turned
        return turned

    def store(g, t, part):
        if t is None:
            copy(g).start()
        else:
            here = slice(t * LANES, (t + 1) * LANES)
            out_ref[g, :, here] = x_ref[g, :, here] - part

    decode(
        groups, numbers_of, lambda g: side(rep_ref, mine_ref, other_ref, g), w_ref,
        number_ref, high_ref, low_ref, dense_ref, store, False,
    )
    for g in range(groups):
        copy(g).wait()


def total_kernel(a_ref, b_ref, c_ref, d_ref, after_ref, out_ref):
    out_ref[...] = (a_ref[...] + b_ref[...]) + (c_ref[...] + d_ref[...])


def energy_kernel(replicas, a_ref, b_ref, out_ref, done_ref):
    square = jnp.square(a_ref[...] / replicas) + jnp.square(b_ref[...] / replicas)
    energy = jnp.sum(jnp.sum(square, axis=0, keepdims=True), axis=1, keepdims=True)
    out_ref[...] = jnp.broadcast_to(energy[None], out_ref.shape)
    done_ref[...] = jnp.broadcast_to(energy, done_ref.shape)


def raw_kernel(
    rep_ref, flip_ref, mine_ref, other_ref, w_ref, after_ref, near_ref, far_hbm,
    number_ref, high_ref, low_ref, dense_ref, out_ref, sem,
):
    near = near_ref.shape[0]
    groups = near + out_ref.shape[0]

    def copy(i):
        return pltpu.make_async_copy(out_ref.at[i], far_hbm.at[i], sem.at[i])

    def store(g, t, part):
        far = groups - 1 - g
        if t is None:
            copy(far).start() if g >= near else None
        elif g >= near:
            out_ref[far, :, t * LANES : (t + 1) * LANES] = part
        else:
            near_ref[g, :, t * LANES : (t + 1) * LANES] = part

    decode(
        groups, lambda g: flip_ref[g], lambda g: side(rep_ref, mine_ref, other_ref, g), w_ref,
        number_ref, high_ref, low_ref, dense_ref, store, True,
    )
    for i in range(groups - near):
        copy(i).wait()


def update_kernel(entries, replicas, near_ref, far_hbm, energy_ref, out_hbm, far_ref, out_ref, far_sem, sem):
    groups = out_ref.shape[0]
    near = near_ref.shape[0]

    def fetch(i):
        return pltpu.make_async_copy(far_hbm.at[i], far_ref.at[i], far_sem.at[i])

    def copy(g):
        return pltpu.make_async_copy(out_ref.at[g], out_hbm.at[:, columns(g)], sem.at[g])

    for i in range(groups - near):
        fetch(i).start()
    energy = jnp.sum(energy_ref[:, 0, :], axis=0, keepdims=True)
    scale = lax.rsqrt(energy / entries + 1e-06) / replicas
    scale = jnp.concatenate([scale] * TILES, axis=1)

    def near_body(g, carry):
        out_ref[g] = (near_ref[g] * scale).astype(BF)
        copy(g).start()
        return carry

    def far_body(i, carry):
        fetch(i).wait()
        g = groups - 1 - i
        out_ref[g] = (far_ref[i] * scale).astype(BF)
        copy(g).start()
        return carry

    lax.fori_loop(0, near, near_body, 0)
    lax.fori_loop(0, groups - near, far_body, 0)
    for g in range(groups):
        copy(g).wait()


def call(kernel, name, operands, out_shape, scratch=(), microseconds=1.0):
    specs, arrays = [], []
    for place, array in operands:
        specs.append(pl.BlockSpec(memory_space=place))
        arrays.append(pltpu.with_memory_space_constraint(array, place) if place is pltpu.HBM else array)
    shapes = out_shape if isinstance(out_shape, list) else [out_shape]
    outs = [
        pl.BlockSpec(memory_space=pltpu.HBM if shape.memory_space is pltpu.HBM else pltpu.VMEM)
        for shape in shapes
    ]
    return pl.pallas_call(
        kernel,
        in_specs=specs,
        out_specs=outs if isinstance(out_shape, list) else outs[0],
        out_shape=out_shape,
        scratch_shapes=list(scratch),
        compiler_params=pltpu.CompilerParams(vmem_limit_bytes=VMEM_BYTES),
        cost_estimate=pl.CostEstimate(
            flops=0, bytes_accessed=int(microseconds * 3.0e6), transcendentals=0
        ),
        name=name,
    )(*arrays)


def per_device(momentum, kept, counts):
    _, rows, width = momentum.shape
    blocks = width // CH
    groups = width // WIDTH
    half = groups // 2
    replicas = lax.axis_size("rep")
    shards = lax.axis_size("fsdp")
    rep = lax.axis_index("rep").astype(jnp.int32).reshape(1)
    basis = pair_table()
    forward = jnp.asarray(split_weights(basis.T))
    inverse = jnp.asarray(split_weights(basis))
    hbm, vmem, smem = pltpu.HBM, pltpu.VMEM, pltpu.SMEM
    half_shape = (half, rows, LANES)
    flat = (half * rows, LANES)
    dma = pltpu.SemaphoreType.DMA
    turned = [vmem((2, LANES, LANES), jnp.float32)] * 3 + [vmem((2, TILES * rows, 2 * LANES), BF)]

    numbers, mine, other, x = call(
        pick_kernel,
        "pick",
        [
            (smem, rep),
            (hbm, momentum),
            (hbm, jnp.transpose(kept, (0, 2, 1))),
            (hbm, counts),
            (hbm, forward),
        ],
        [
            vmem((groups, rows, LANES), jnp.int32),
            vmem(half_shape, jnp.float32),
            vmem(half_shape, jnp.float32),
            vmem((groups, rows, WIDTH), jnp.float32),
        ],
        [
            vmem((rows, KEEP, blocks), jnp.int32),
            vmem((rows, blocks), jnp.int32),
            vmem(forward.shape, BF),
            vmem((groups, rows, LANES), jnp.float32),
            vmem((2, TILES, rows, LANES), jnp.float32),
            dma((3,)),
            dma((groups,)),
        ],
        5.0,
    )

    swap = [(i, i ^ 1) for i in range(replicas)]
    chip = mine.reshape(flat) + lax.ppermute(other.reshape(flat), "rep", swap)
    away = []
    for step in (4, 2, 6):
        ring = [(i, (i + step) % replicas) for i in range(replicas)]
        away.append(lax.ppermute(chip, "rep", ring))
    new_moment, flipped = call(
        residue_kernel,
        "residue",
        [
            (smem, rep),
            (vmem, x),
            (vmem, numbers),
            (vmem, mine),
            (vmem, other),
            (vmem, inverse),
            (vmem, chip),
        ],
        [hbm(momentum.shape, jnp.float32), vmem((groups, LANES, LANES), jnp.float32)],
        turned + [vmem((groups, rows, WIDTH), jnp.float32), dma((groups,))],
        5.0,
    )
    total = call(
        total_kernel,
        "total",
        [(vmem, chip)] + [(vmem, part) for part in away] + [(vmem, flipped)],
        vmem(flat, jnp.float32),
        microseconds=0.5,
    )
    total_other = lax.ppermute(total, "rep", swap)
    own_energy, done = call(
        functools.partial(energy_kernel, replicas),
        "energy",
        [(vmem, total), (vmem, total_other)],
        [vmem((shards, 1, LANES), jnp.float32), vmem((8, LANES), jnp.float32)],
        microseconds=0.5,
    )
    energies = lax.all_to_all(own_energy, "fsdp", 0, 0, tiled=True)
    far = groups - half
    near_raw, far_raw = call(
        raw_kernel,
        "raw",
        [
            (smem, rep),
            (vmem, flipped),
            (vmem, total.reshape(half_shape)),
            (vmem, total_other.reshape(half_shape)),
            (vmem, inverse),
            (vmem, done),
        ],
        [vmem((half, rows, WIDTH), jnp.float32), hbm((far, rows, WIDTH), jnp.float32)],
        turned + [vmem((far, rows, WIDTH), jnp.float32), dma((far,))],
        5.0,
    )
    update = call(
        functools.partial(update_kernel, rows * width * shards, replicas),
        "update",
        [(vmem, near_raw), (hbm, far_raw), (vmem, energies)],
        hbm((rows, width), BF),
        [vmem((far, rows, WIDTH), jnp.float32), vmem((groups, rows, WIDTH), BF), dma((far,)), dma((groups,))],
        2.0,
    )
    return new_moment, update


def solution(mesh):
    placed = (P("rep", "fsdp", None), P("fsdp", None, None), P(None, "fsdp", None))
    return jax.shard_map(
        per_device,
        mesh=mesh,
        in_specs=placed,
        out_specs=(P("rep", "fsdp", None), P("fsdp", None)),
        check_vma=False,
    )
```

time: 49 us -> 46.8 us (0.955)
  blocking collectives: 19.4 us -> 0 us
  starting transfers between devices: 8.71 us -> 19.7 us
  waiting for transfers between devices: 3.62 us -> 8.33 us
  Pallas kernels: 16.5 us -> 17.9 us
    all_to_all x1 -> x0, blocking collectives: 19.4 us -> none  [per_device(): energies = lax.all_to_all(energies, 'fsdp', 0, 0, tiled=True)]
    all_to_all x0 -> x1, starting transfers between devices: none -> 11 us  [per_device(): energies = lax.all_to_all(own_energy, 'fsdp', 0, 0, tiled=True)]
    all_to_all x0 -> x1, waiting for transfers between devices: none -> 4.42 us  [per_device(): energies = lax.all_to_all(own_energy, 'fsdp', 0, 0, tiled=True)]
    pallas_call x5 -> x6, Pallas kernels: 16.5 us -> 17.9 us  [call(): pl.pallas_call(kernel, in_specs=specs, out_specs=outs if isinstance(out_s...]
  transfers between devices with their start and end apart: 5 -> 6, of which waited for: 4 -> 5; matrix products, arithmetic and copies ran while one was open for 0% -> 0% of each run, Pallas kernels for 10% -> 18%
where the time goes in v3:
time: 46.8 us; the launch traced here: 46.7 us
  starting transfers between devices  19.7 us (42%)
  Pallas kernels  17.9 us (38%)
  waiting for transfers between devices  8.33 us (18%)
  between operations  0.7 us (1%)
    pallas_call x6, Pallas kernels, call(): pl.pallas_call(kernel, in_specs=specs, out_specs=outs if isinstance(out_s...  17.9 us
    all_to_all x1, starting transfers between devices, per_device(): energies = lax.all_to_all(own_energy, 'fsdp', 0, 0, tiled=True)  11 us
    all_to_all x1, waiting for transfers between devices, per_device(): energies = lax.all_to_all(own_energy, 'fsdp', 0, 0, tiled=True)  4.42 us
    ppermute x1, starting transfers between devices, per_device(): chip = mine.reshape(flat) + lax.ppermute(other.reshape(flat), 'rep', swap)  3.33 us
    ppermute x3, starting transfers between devices, per_device(): away.append(lax.ppermute(chip, 'rep', ring))  2.72 us
    ppermute x1, starting transfers between devices, per_device(): total_other = lax.ppermute(total, 'rep', swap)  2.64 us
    ppermute x3, waiting for transfers between devices, per_device(): away.append(lax.ppermute(chip, 'rep', ring))  1.9 us
    ppermute x1, waiting for transfers between devices, per_device(): total_other = lax.ppermute(total, 'rep', swap)  1.01 us
  transfers between devices with their start and end apart: 6, of which 5 were waited for; matrix products, arithmetic and copies ran while one was open for 0% of the time, Pallas kernels for 18%

profile of v3, /device:TPU:1, one launch (start us, length us, event | category | flops | bytes accessed | tf_op | source)
XLA Modules:
  0.0 46.7 jit_solution(9423884241016896766)
XLA Ops:
  0.6 0.0 copy-start
  0.6 5.6 %pick.1 = (s32[6,96,128]{2,1,0:T(8,128)S(1)}, f32[3,96,128]{2,1,0:T(8,128)S(1)}, f32[3,96,128]{2,1,0:T(8,128)S(1)}, f32[6,96,2048]{2,1,0:T(8,128)S(1)}) custom-call(s32[1]{0:T(128)} %bitcast.rep_ref, f32[1,96,12288]{2,1,0:T(8,128)} %x_hbm.1, s32[96,4,192]{2,1,0:T(4,128)} %bitcast.10, s32[8,96,192]{2,1,0:T(8,128)} %cnt_hbm.1, ...), custom_call_target="tpu_custom_call" | custom-call | bytes 15000000 | tf_op jit(solution)/shard_map/pick/pallas_call | solution.py:346
  6.3 3.3 %collective-permute-start = (f32[288,128]{1,0:T(8,128)S(1)}, f32[288,128]{1,0:T(8,128)S(1)}, u32[]{:S(2)}, u32[]{:S(2)}) collective-permute-start(f32[288,128]{1,0:T(8,128)S(1)} %bitcast.9), channel_id=1, source_target_pairs={{0,32},{32,0},{64,96},{96,64},{128,160},{160,128},{192,224},{224,1... | collective-permute-start | bytes 442376 | tf_op jit(solution)/shard_map/ppermute | solution.py:406
  9.6 1.0 %collective-permute-done = f32[288,128]{1,0:T(8,128)S(1)} collective-permute-done((f32[288,128]{1,0:T(8,128)S(1)}, f32[288,128]{1,0:T(8,128)S(1)}, u32[]{:S(2)}, u32[]{:S(2)}) %collective-permute-start) | collective-permute-done | bytes 147488 | tf_op jit(solution)/shard_map/ppermute | solution.py:406
  10.6 1.1 %collective-permute-start.3 = (f32[288,128]{1,0:T(8,128)S(1)}, f32[288,128]{1,0:T(8,128)S(1)}, u32[]{:S(2)}, u32[]{:S(2)}) collective-permute-start(f32[288,128]{1,0:T(8,128)S(1)} %bitcast_add_fusion.after_ref.a_ref), channel_id=1, source_target_pairs={{0,192},{32,224},{64,0},{96,32},{128,64},{160,96},{192,128},{224,1... | collective-permute-start | bytes 442376 | tf_op jit(solution)/shard_map/ppermute | solution.py:410
  11.7 0.5 collective-permute-start.2
  12.2 1.2 %collective-permute-start.1 = (f32[288,128]{1,0:T(8,128)S(1)}, f32[288,128]{1,0:T(8,128)S(1)}, u32[]{:S(2)}, u32[]{:S(2)}) collective-permute-start(f32[288,128]{1,0:T(8,128)S(1)} %bitcast_add_fusion.after_ref.a_ref), channel_id=1, source_target_pairs={{0,128},{32,160},{64,192},{96,224},{128,0},{160,32},{192,64},{224,... | collective-permute-start | bytes 442376 | tf_op jit(solution)/shard_map/ppermute | solution.py:410
  13.3 0.0 copy-done
  13.3 4.5 %residue.1 = (f32[1,96,12288]{2,1,0:T(8,128)}, f32[6,128,128]{2,1,0:T(8,128)S(1)}) custom-call(s32[1]{0:T(128)} %bitcast.rep_ref, f32[6,96,2048]{2,1,0:T(8,128)S(1)} %get-tuple-element.12.x_ref, s32[6,96,128]{2,1,0:T(8,128)S(1)} %get-tuple-element.13.chosen_ref, f32[3,96,128]{2,1,0:T(8,128)S(1)} %get-tuple-element.14.mine_ref, ...), custom_call_target="tpu_custom_call" | custom-call | bytes 15000000 | tf_op jit(solution)/shard_map/residue/pallas_call | solution.py:346
  17.9 0.0 collective-permute-done.3.d_ref
  17.9 0.9 %collective-permute-done.2.c_ref = f32[288,128]{1,0:T(8,128)S(1)} collective-permute-done((f32[288,128]{1,0:T(8,128)S(1)}, f32[288,128]{1,0:T(8,128)S(1)}, u32[]{:S(2)}, u32[]{:S(2)}) %collective-permute-start.2) | collective-permute-done | bytes 147488 | tf_op jit(solution)/shard_map/ppermute | solution.py:410
  18.8 1.0 %collective-permute-done.1.b_ref = f32[288,128]{1,0:T(8,128)S(1)} collective-permute-done((f32[288,128]{1,0:T(8,128)S(1)}, f32[288,128]{1,0:T(8,128)S(1)}, u32[]{:S(2)}, u32[]{:S(2)}) %collective-permute-start.1) | collective-permute-done | bytes 147488 | tf_op jit(solution)/shard_map/ppermute | solution.py:410
  19.8 2.6 %collective-permute-start.4 = (f32[288,128]{1,0:T(8,128)S(1)}, f32[288,128]{1,0:T(8,128)S(1)}, u32[]{:S(2)}, u32[]{:S(2)}) collective-permute-start(f32[288,128]{1,0:T(8,128)S(1)} %total.1.a_ref), channel_id=1, source_target_pairs={{0,32},{32,0},{64,96},{96,64},{128,160},{160,128},{192,224},{224,1... | collective-permute-start | bytes 442376 | tf_op jit(solution)/shard_map/ppermute | solution.py:434
  22.5 1.0 %collective-permute-done.4.b_ref = f32[288,128]{1,0:T(8,128)S(1)} collective-permute-done((f32[288,128]{1,0:T(8,128)S(1)}, f32[288,128]{1,0:T(8,128)S(1)}, u32[]{:S(2)}, u32[]{:S(2)}) %collective-permute-start.4) | collective-permute-done | bytes 147488 | tf_op jit(solution)/shard_map/ppermute | solution.py:434
  23.5 0.7 %energy.1 = (f32[32,1,128]{2,1,0:T(1,128)}, f32[8,128]{1,0:T(8,128)S(1)}) custom-call(f32[288,128]{1,0:T(8,128)S(1)} %total.1.a_ref, f32[288,128]{1,0:T(8,128)S(1)} %collective-permute-done.4.b_ref), custom_call_target="tpu_custom_call" | custom-call | bytes 1500000 | tf_op jit(solution)/shard_map/energy/pallas_call | solution.py:346
  24.2 11.0 %all-to-all-start = ((f32[32,1,128]{2,1,0:T(1,128)}), f32[32,1,128]{2,1,0:T(1,128)S(1)}, u32[]{:S(2)}, u32[]{:S(2)}) async-start(f32[32,1,128]{2,1,0:T(1,128)} %get-tuple-element.21), calls=%async_computation | async-start | bytes 32768 | tf_op jit(solution)/shard_map/all_to_all | solution.py:442
  35.2 4.1 %raw.1 = (f32[3,96,2048]{2,1,0:T(8,128)S(1)}, f32[3,96,2048]{2,1,0:T(8,128)}) custom-call(s32[1]{0:T(128)} %bitcast.rep_ref, f32[6,128,128]{2,1,0:T(8,128)S(1)} %get-tuple-element.17.after_ref.flip_ref, f32[3,96,128]{2,1,0:T(8,128)S(1)} %bitcast.7, f32[3,96,128]{2,1,0:T(8,128)S(1)} %bitcast.8, bf16[256,256]{1,0:T(8,128)(2,1)S(1)} %copy-done, ...), custom_call_target="tpu_custom_call" | custom-call | bytes 15000000 | tf_op jit(solution)/shard_map/raw/pallas_call | solution.py:346
  39.3 4.4 %all-to-all-done.energy_ref = f32[32,1,128]{2,1,0:T(1,128)S(1)} async-done(((f32[32,1,128]{2,1,0:T(1,128)}), f32[32,1,128]{2,1,0:T(1,128)S(1)}, u32[]{:S(2)}, u32[]{:S(2)}) %all-to-all-start) | async-done | bytes 16416 | tf_op jit(solution)/shard_map/all_to_all | solution.py:442
  43.8 2.9 %update.1 = bf16[96,12288]{1,0:T(8,128)(2,1)} custom-call(f32[3,96,2048]{2,1,0:T(8,128)S(1)} %get-tuple-element.19.near_ref, f32[3,96,2048]{2,1,0:T(8,128)} %get-tuple-element.20.far_hbm, f32[32,1,128]{2,1,0:T(1,128)S(1)} %all-to-all-done.energy_ref), custom_call_target="tpu_custom_call" | custom-call | bytes 6000000 | tf_op jit(solution)/shard_map/update/pallas_call | solution.py:346
  (2 shorter events, 0.0 us)
Async XLA Ops:
  0.6 12.7 %copy-start = (bf16[256,256]{1,0:T(8,128)(2,1)S(1)}, bf16[256,256]{1,0:T(8,128)(2,1)}, u32[]{:S(2)}) copy-start(bf16[256,256]{1,0:T(8,128)(2,1)} %constant.11.clone.w_ref) | copy-start | bytes 393220
  6.3 4.3 %collective-permute-start = (f32[288,128]{1,0:T(8,128)S(1)}, f32[288,128]{1,0:T(8,128)S(1)}, u32[]{:S(2)}, u32[]{:S(2)}) collective-permute-start(f32[288,128]{1,0:T(8,128)S(1)} %bitcast.9), channel_id=1, source_target_pairs={{0,32},{32,0},{64,96},{96,64},{128,160},{160,128},{192,224},{224,1... | collective-permute-start | bytes 442376 | tf_op jit(solution)/shard_map/ppermute | solution.py:406
  10.6 7.3 %collective-permute-start.3 = (f32[288,128]{1,0:T(8,128)S(1)}, f32[288,128]{1,0:T(8,128)S(1)}, u32[]{:S(2)}, u32[]{:S(2)}) collective-permute-start(f32[288,128]{1,0:T(8,128)S(1)} %bitcast_add_fusion.after_ref.a_ref), channel_id=1, source_target_pairs={{0,192},{32,224},{64,0},{96,32},{128,64},{160,96},{192,128},{224,1... | collective-permute-start | bytes 442376 | tf_op jit(solution)/shard_map/ppermute | solution.py:410
  11.7 7.1 %collective-permute-start.2 = (f32[288,128]{1,0:T(8,128)S(1)}, f32[288,128]{1,0:T(8,128)S(1)}, u32[]{:S(2)}, u32[]{:S(2)}) collective-permute-start(f32[288,128]{1,0:T(8,128)S(1)} %bitcast_add_fusion.after_ref.a_ref), channel_id=1, source_target_pairs={{0,64},{32,96},{64,128},{96,160},{128,192},{160,224},{192,0},{224,... | collective-permute-start | bytes 442376 | tf_op jit(solution)/shard_map/ppermute | solution.py:410
  12.2 7.6 %collective-permute-start.1 = (f32[288,128]{1,0:T(8,128)S(1)}, f32[288,128]{1,0:T(8,128)S(1)}, u32[]{:S(2)}, u32[]{:S(2)}) collective-permute-start(f32[288,128]{1,0:T(8,128)S(1)} %bitcast_add_fusion.after_ref.a_ref), channel_id=1, source_target_pairs={{0,128},{32,160},{64,192},{96,224},{128,0},{160,32},{192,64},{224,... | collective-permute-start | bytes 442376 | tf_op jit(solution)/shard_map/ppermute | solution.py:410
  19.8 3.6 %collective-permute-start.4 = (f32[288,128]{1,0:T(8,128)S(1)}, f32[288,128]{1,0:T(8,128)S(1)}, u32[]{:S(2)}, u32[]{:S(2)}) collective-permute-start(f32[288,128]{1,0:T(8,128)S(1)} %total.1.a_ref), channel_id=1, source_target_pairs={{0,32},{32,0},{64,96},{96,64},{128,160},{160,128},{192,224},{224,1... | collective-permute-start | bytes 442376 | tf_op jit(solution)/shard_map/ppermute | solution.py:434
  24.2 19.6 %all-to-all-start = ((f32[32,1,128]{2,1,0:T(1,128)}), f32[32,1,128]{2,1,0:T(1,128)S(1)}, u32[]{:S(2)}, u32[]{:S(2)}) async-start(f32[32,1,128]{2,1,0:T(1,128)} %get-tuple-element.21), calls=%async_computation | async-start | bytes 32768 | tf_op jit(solution)/shard_map/all_to_all | solution.py:442

commit v4 on v3

--- a/solution.py
+++ b/solution.py
@@ -75,12 +75,46 @@
     return pl.ds(pl.multiple_of(group * WIDTH, WIDTH), WIDTH)
 
 
-def pick_kernel(
-    rep_ref, x_hbm, kept_hbm, cnt_hbm, w_hbm, number_ref, mine_ref, other_ref, x_ref,
-    kept_ref, cnt_ref, w_ref, live_ref, coeff_ref, small_sem, x_sem,
+def choose_groups(x_ref, number_ref, live_ref, w_ref, coeff_ref, out_ref, first_group):
+    count, rows, _ = out_ref.shape
+    lanes = lane_ids(8)
+    block_start = lanes % PAIR * CH
+    tile_of = lanes % CELLS // PAIR
+
+    def transform(i, buffer, tiles):
+        g = first_group + i
+        parts = [
+            jnp.concatenate(halves(x_ref[g, :, t * LANES : (t + 1) * LANES]), axis=1) for t in tiles
+        ]
+        for t, coeffs in zip(tiles, apply_weights(parts, w_ref[...])):
+            coeff_ref[buffer, t] = coeffs
+
+    def choose(i, buffer, first):
+        here = slice(first, first + 8)
+        index = number_ref[first_group + i, here] + block_start
+        picked = jnp.zeros((8, LANES), jnp.float32)
+        for t in range(TILES):
+            picked = jnp.where(tile_of == t, lane_gather(coeff_ref[buffer, t, here], index), picked)
+        out_ref[i, here] = jnp.where(live_ref[first_group + i, here] > 0.0, picked, 0.0)
+
+    transform(0, 0, range(TILES))
+    for i in range(count - 1):
+        for j in range(CHUNKS):
+            transform(i + 1, (i + 1) % 2, span(TILES, j))
+            for part in span(rows // 8, j):
+                choose(i, i % 2, 8 * part)
+    for part in range(rows // 8):
+        choose(count - 1, (count - 1) % 2, 8 * part)
+
+
+def pick_other_kernel(
+    rep_ref, x_hbm, kept_hbm, cnt_hbm, w_hbm, number_ref, live_ref, other_ref, x_ref,
+    kept_ref, cnt_ref, w_ref, coeff_ref, small_sem, x_sem,
 ):
     groups, rows, _ = x_ref.shape
     half = groups // 2
+    core = rep_ref[0] % 2
+    theirs, ours = (1 - core) * half, core * half
     small = [
         pltpu.make_async_copy(w_hbm, w_ref, small_sem.at[0]),
         pltpu.make_async_copy(kept_hbm, kept_ref, small_sem.at[1]),
@@ -89,13 +123,18 @@
     for copy in small:
         copy.start()
 
-    def x_copy(g):
+    def x_copy(first, i):
+        g = first + i
         return pltpu.make_async_copy(x_hbm.at[0, :, columns(g)], x_ref.at[g], x_sem.at[g])
 
-    for g in range(groups):
-        x_copy(g).start()
+    for i in range(half):
+        x_copy(theirs, i).start()
     for copy in small:
         copy.wait()
+    for i in range(half):
+        x_copy(theirs, i).wait()
+    for i in range(half):
+        x_copy(ours, i).start()
 
     slot = lane_ids(rows) // CELLS
     counts = cnt_ref[...]
@@ -107,50 +146,14 @@
         number_ref[g] = chosen
         live_ref[g] = jnp.where(slot < spread(counts, g, rows), 1.0, 0.0)
 
-    lanes = lane_ids(8)
-    block_start = lanes % PAIR * CH
-    tile_of = lanes % CELLS // PAIR
-    core = rep_ref[0] % 2
-
-    def transform(g, buffer, tiles):
-        parts = [
-            jnp.concatenate(halves(x_ref[g, :, t * LANES : (t + 1) * LANES]), axis=1) for t in tiles
-        ]
-        for t, coeffs in zip(tiles, apply_weights(parts, w_ref[...])):
-            coeff_ref[buffer, t] = coeffs
-
-    def choose(g, buffer, first):
-        here = slice(first, first + 8)
-        index = number_ref[g, here] + block_start
-        picked = jnp.zeros((8, LANES), jnp.float32)
-        for t in range(TILES):
-            picked = jnp.where(tile_of == t, lane_gather(coeff_ref[buffer, t, here], index), picked)
-        return jnp.where(live_ref[g, here] > 0.0, picked, 0.0)
-
-    def put(g, parts):
-        picked = jnp.concatenate(parts, axis=0)
-
-        @pl.when(g // half == core)
-        def _():
-            mine_ref[g % half] = picked
-
-        @pl.when(g // half != core)
-        def _():
-            other_ref[g % half] = picked
-
-    def step(g, buffer):
-        x_copy(g + 1).wait()
-        parts = []
-        for j in range(CHUNKS):
-            transform(g + 1, 1 - buffer, span(TILES, j))
-            parts += [choose(g, buffer, 8 * i) for i in span(rows // 8, j)]
-        put(g, parts)
-
-    x_copy(0).wait()
-    transform(0, 0, range(TILES))
-    two_by_two(step, groups - 1)
-    last = groups - 1
-    put(last, [choose(last, last % 2, first) for first in range(0, rows, 8)])
+    choose_groups(x_ref, number_ref, live_ref, w_ref, coeff_ref, other_ref, theirs)
+    for i in range(half):
+        x_copy(ours, i).wait()
+
+
+def pick_mine_kernel(rep_ref, x_ref, number_ref, live_ref, w_ref, mine_ref, coeff_ref):
+    first = rep_ref[0] % 2 * mine_ref.shape[0]
+    choose_groups(x_ref, number_ref, live_ref, w_ref, coeff_ref, mine_ref, first)
 
 
 def span(count, j):
@@ -233,36 +236,52 @@
 
 
 def residue_kernel(
-    rep_ref, x_ref, chosen_ref, mine_ref, other_ref, w_ref, after_ref, out_hbm, flip_ref,
-    number_ref, high_ref, low_ref, dense_ref, out_ref, sem,
+    first, rep_ref, x_ref, chosen_ref, mine_ref, other_ref, w_ref, after_ref, *refs
 ):
-    groups = x_ref.shape[0]
-
-    def copy(g):
-        return pltpu.make_async_copy(out_ref.at[g], out_hbm.at[0, :, columns(g)], sem.at[g])
-
-    def numbers_of(g):
-        turned = flip(chosen_ref[g].astype(jnp.float32))
-        flip_ref[g] = turned
+    (
+        out_hbm, flip_hbm, done_ref, number_ref, high_ref, low_ref, dense_ref, out_ref, flip_ref, sem, flip_sem,
+    ) = refs[-11:]
+    count = out_ref.shape[0]
+    done_ref[...] = jnp.zeros(done_ref.shape, jnp.float32)
+
+    def copy(i):
+        return pltpu.make_async_copy(out_ref.at[i], out_hbm.at[0, :, columns(first + i)], sem.at[i])
+
+    def flip_copy(i):
+        return pltpu.make_async_copy(flip_ref.at[i], flip_hbm.at[i], flip_sem.at[i])
+
+    def numbers_of(i):
+        turned = flip(chosen_ref[first + i].astype(jnp.float32))
+        flip_ref[i] = turned
+        flip_copy(i).start()
         return turned
 
-    def store(g, t, part):
+    def store(i, t, part):
         if t is None:
-            copy(g).start()
+            copy(i).start()
         else:
             here = slice(t * LANES, (t + 1) * LANES)
-            out_ref[g, :, here] = x_ref[g, :, here] - part
+            out_ref[i, :, here] = x_ref[first + i, :, here] - part
 
     decode(
-        groups, numbers_of, lambda g: side(rep_ref, mine_ref, other_ref, g), w_ref,
+        count, numbers_of, lambda i: side(rep_ref, mine_ref, other_ref, first + i), w_ref,
         number_ref, high_ref, low_ref, dense_ref, store, False,
     )
-    for g in range(groups):
-        copy(g).wait()
-
-
-def total_kernel(a_ref, b_ref, c_ref, d_ref, after_ref, out_ref):
-    out_ref[...] = (a_ref[...] + b_ref[...]) + (c_ref[...] + d_ref[...])
+    for i in range(count):
+        copy(i).wait()
+        flip_copy(i).wait()
+
+
+def add_kernel(*refs, counts):
+    refs = list(refs)
+    left, right = [[refs.pop(0) for _ in range(count)] for count in counts[:2]]
+    outs = refs[len(refs) - counts[2] :]
+    left, right = [jnp.concatenate([ref[...] for ref in part], axis=0) for part in (left, right)]
+    total = left + right
+    at = 0
+    for out in outs:
+        out[...] = total[at : at + out.shape[0]]
+        at += out.shape[0]
 
 
 def energy_kernel(replicas, a_ref, b_ref, out_ref, done_ref):
@@ -273,11 +292,20 @@
 
 
 def raw_kernel(
-    rep_ref, flip_ref, mine_ref, other_ref, w_ref, after_ref, near_ref, far_hbm,
-    number_ref, high_ref, low_ref, dense_ref, out_ref, sem,
+    rep_ref, low_flip_hbm, high_flip_hbm, mine_ref, other_ref, w_hbm, after_ref, near_ref, far_hbm,
+    number_ref, high_ref, low_ref, dense_ref, out_ref, flip_ref, w_ref, sem, in_sem,
 ):
     near = near_ref.shape[0]
     groups = near + out_ref.shape[0]
+    fetches = [
+        pltpu.make_async_copy(low_flip_hbm, flip_ref.at[: groups // 2], in_sem.at[0]),
+        pltpu.make_async_copy(high_flip_hbm, flip_ref.at[groups // 2 :], in_sem.at[1]),
+        pltpu.make_async_copy(w_hbm, w_ref, in_sem.at[2]),
+    ]
+    for fetch in fetches:
+        fetch.start()
+    for fetch in fetches:
+        fetch.wait()
 
     def copy(i):
         return pltpu.make_async_copy(out_ref.at[i], far_hbm.at[i], sem.at[i])
@@ -333,7 +361,7 @@
         copy(g).wait()
 
 
-def call(kernel, name, operands, out_shape, scratch=(), microseconds=1.0):
+def call(kernel, name, operands, out_shape, scratch=(), microseconds=1.0, aliases=()):
     specs, arrays = [], []
     for place, array in operands:
         specs.append(pl.BlockSpec(memory_space=place))
@@ -349,6 +377,7 @@
         out_specs=outs if isinstance(out_shape, list) else outs[0],
         out_shape=out_shape,
         scratch_shapes=list(scratch),
+        input_output_aliases=dict(aliases),
         compiler_params=pltpu.CompilerParams(vmem_limit_bytes=VMEM_BYTES),
         cost_estimate=pl.CostEstimate(
             flops=0, bytes_accessed=int(microseconds * 3.0e6), transcendentals=0
@@ -374,9 +403,11 @@
     dma = pltpu.SemaphoreType.DMA
     turned = [vmem((2, LANES, LANES), jnp.float32)] * 3 + [vmem((2, TILES * rows, 2 * LANES), BF)]
 
-    numbers, mine, other, x = call(
-        pick_kernel,
-        "pick",
+    coeffs = vmem((2, TILES, rows, LANES), jnp.float32)
+
+    numbers, live, other, x = call(
+        pick_other_kernel,
+        "pick_other",
         [
             (smem, rep),
             (hbm, momentum),
@@ -386,7 +417,7 @@
         ],
         [
             vmem((groups, rows, LANES), jnp.int32),
-            vmem(half_shape, jnp.float32),
+            vmem((groups, rows, LANES), jnp.float32),
             vmem(half_shape, jnp.float32),
             vmem((groups, rows, WIDTH), jnp.float32),
         ],
@@ -394,45 +425,83 @@
             vmem((rows, KEEP, blocks), jnp.int32),
             vmem((rows, blocks), jnp.int32),
             vmem(forward.shape, BF),
-            vmem((groups, rows, LANES), jnp.float32),
-            vmem((2, TILES, rows, LANES), jnp.float32),
+            coeffs,
             dma((3,)),
             dma((groups,)),
         ],
-        5.0,
+        4.0,
+    )
+    mine = call(
+        pick_mine_kernel,
+        "pick_mine",
+        [(smem, rep), (vmem, x), (vmem, numbers), (vmem, live), (vmem, forward)],
+        vmem(half_shape, jnp.float32),
+        [coeffs],
+        2.0,
     )
 
     swap = [(i, i ^ 1) for i in range(replicas)]
-    chip = mine.reshape(flat) + lax.ppermute(other.reshape(flat), "rep", swap)
-    away = []
-    for step in (4, 2, 6):
-        ring = [(i, (i + step) % replicas) for i in range(replicas)]
-        away.append(lax.ppermute(chip, "rep", ring))
-    new_moment, flipped = call(
-        residue_kernel,
-        "residue",
-        [
-            (smem, rep),
-            (vmem, x),
-            (vmem, numbers),
-            (vmem, mine),
-            (vmem, other),
-            (vmem, inverse),
-            (vmem, chip),
-        ],
-        [hbm(momentum.shape, jnp.float32), vmem((groups, LANES, LANES), jnp.float32)],
-        turned + [vmem((groups, rows, WIDTH), jnp.float32), dma((groups,))],
-        5.0,
-    )
-    total = call(
-        total_kernel,
-        "total",
-        [(vmem, chip)] + [(vmem, part) for part in away] + [(vmem, flipped)],
-        vmem(flat, jnp.float32),
-        microseconds=0.5,
-    )
+    pieces = 1
+    piece = vmem((flat[0] // pieces, LANES), jnp.float32)
+
+    def add(name, left, right, after, out):
+        counts = (len(left), len(right), len(out))
+        return list(
+            call(
+                functools.partial(add_kernel, counts=counts),
+                name,
+                [(vmem, array) for array in left + right + after],
+                out,
+                microseconds=0.3,
+            )
+        )
+
+    partner = lax.ppermute(other.reshape(flat), "rep", swap)
+    total = add("chip", [mine.reshape(flat)], [partner], [], [piece] * pieces)
+    new_moment = None
+    flips = []
+    for part in range(2):
+        pairs = []
+        for y in range(replicas // 2):
+            for core in range(2):
+                there = y ^ 1 if part == core else (y + (1 if y % 2 else -1)) % (replicas // 2)
+                pairs.append((2 * y + core, 2 * there + core))
+        arrived = [lax.ppermute(some, "rep", pairs) for some in total]
+        earlier = [] if new_moment is None else [(hbm, new_moment)]
+        new_moment, flipped, done = call(
+            functools.partial(residue_kernel, part * half),
+            f"residue_{part}",
+            [
+                (smem, rep),
+                (vmem, x),
+                (vmem, numbers),
+                (vmem, mine),
+                (vmem, other),
+                (vmem, inverse),
+                (vmem, total[0]),
+            ]
+            + earlier,
+            [
+                hbm(momentum.shape, jnp.float32),
+                hbm((half, LANES, LANES), jnp.float32),
+                vmem((8, LANES), jnp.float32),
+            ],
+            turned
+            + [
+                vmem((half, rows, WIDTH), jnp.float32),
+                vmem((half, LANES, LANES), jnp.float32),
+                dma((half,)),
+                dma((half,)),
+            ],
+            2.5,
+            {7: 0} if earlier else {},
+        )
+        flips.append(flipped)
+        out = [vmem(flat, jnp.float32)] if part else [piece] * pieces
+        total = add(f"sum_{part}", total, arrived, [done], out)
+    (total,) = total
     total_other = lax.ppermute(total, "rep", swap)
-    own_energy, done = call(
+    own_energy, summed = call(
         functools.partial(energy_kernel, replicas),
         "energy",
         [(vmem, total), (vmem, total_other)],
@@ -440,20 +509,29 @@
         microseconds=0.5,
     )
     energies = lax.all_to_all(own_energy, "fsdp", 0, 0, tiled=True)
-    far = groups - half
+    near = groups * 2 // 3
+    far = groups - near
     near_raw, far_raw = call(
         raw_kernel,
         "raw",
         [
             (smem, rep),
-            (vmem, flipped),
+            (hbm, flips[0]),
+            (hbm, flips[1]),
             (vmem, total.reshape(half_shape)),
             (vmem, total_other.reshape(half_shape)),
-            (vmem, inverse),
-            (vmem, done),
+            (hbm, inverse),
+            (vmem, summed),
         ],
-        [vmem((half, rows, WIDTH), jnp.float32), hbm((far, rows, WIDTH), jnp.float32)],
-        turned + [vmem((far, rows, WIDTH), jnp.float32), dma((far,))],
+        [vmem((near, rows, WIDTH), jnp.float32), hbm((far, rows, WIDTH), jnp.float32)],
+        turned
+        + [
+            vmem((far, rows, WIDTH), jnp.float32),
+            vmem((groups, LANES, LANES), jnp.float32),
+            vmem(inverse.shape, BF),
+            dma((far,)),
+            dma((3,)),
+        ],
         5.0,
     )
     update = call(

time: 46.8 us -> 43.9 us (0.938)
  starting transfers between devices: 19.7 us -> 16.2 us
  Pallas kernels: 17.9 us -> 19.1 us
  waiting for transfers between devices: 8.33 us -> 7.36 us
    all_to_all x1, starting transfers between devices: 11 us -> 9.3 us  [per_device(): energies = lax.all_to_all(own_energy, 'fsdp', 0, 0, tiled=True)]
    ppermute x4 -> x3, starting transfers between devices: 6.06 us -> 4.5 us  [the longest x1 3.33 us: per_device(): partner = lax.ppermute(other.reshape(flat), 'rep', swap)]
    pallas_call x6 -> x10, Pallas kernels: 17.9 us -> 19.1 us  [call(): pl.pallas_call(kernel, in_specs=specs, out_specs=outs if isinstance(out_s...]
    all_to_all x1, waiting for transfers between devices: 4.42 us -> 3.39 us  [per_device(): energies = lax.all_to_all(own_energy, 'fsdp', 0, 0, tiled=True)]
    ppermute x4 -> x3, waiting for transfers between devices: 2.91 us -> 2.96 us  [the longest x2 2.96 us: per_device(): arrived = [lax.ppermute(some, 'rep', pairs) for some in total]]
  transfers between devices with their start and end apart: 6 -> 5, of which waited for: 5 -> 4; matrix products, arithmetic and copies ran while one was open for 0% -> 0% of each run, Pallas kernels for 18% -> 27%
where the time goes in v4:
time: 43.9 us; the launch traced here: 43.4 us
  Pallas kernels  19.1 us (44%)
  starting transfers between devices  16.2 us (37%)
  waiting for transfers between devices  7.36 us (17%)
  between operations  0.73 us (2%)
    pallas_call x10, Pallas kernels, call(): pl.pallas_call(kernel, in_specs=specs, out_specs=outs if isinstance(out_s...  19.1 us
    all_to_all x1, starting transfers between devices, per_device(): energies = lax.all_to_all(own_energy, 'fsdp', 0, 0, tiled=True)  9.3 us
    all_to_all x1, waiting for transfers between devices, per_device(): energies = lax.all_to_all(own_energy, 'fsdp', 0, 0, tiled=True)  3.39 us
    ppermute x1, starting transfers between devices, per_device(): partner = lax.ppermute(other.reshape(flat), 'rep', swap)  3.33 us
    ppermute x2, waiting for transfers between devices, per_device(): arrived = [lax.ppermute(some, 'rep', pairs) for some in total]  2.96 us
    ppermute x1, starting transfers between devices, per_device(): total_other = lax.ppermute(total, 'rep', swap)  2.41 us
    ppermute x2, starting transfers between devices, per_device(): arrived = [lax.ppermute(some, 'rep', pairs) for some in total]  1.17 us
    ppermute x1, waiting for transfers between devices, per_device(): total_other = lax.ppermute(total, 'rep', swap)  1.01 us
  transfers between devices with their start and end apart: 5, of which 4 were waited for; matrix products, arithmetic and copies ran while one was open for 0% of the time, Pallas kernels for 27%

profile of v4, /device:TPU:1, one launch (start us, length us, event | category | flops | bytes accessed | tf_op | source)
XLA Modules:
  0.0 43.4 jit_solution(5979843269134008564)
XLA Ops:
  0.6 0.0 copy-start.1
  0.6 0.0 copy-start
  0.7 3.6 %pick_other.1 = (s32[6,96,128]{2,1,0:T(8,128)S(1)}, f32[6,96,128]{2,1,0:T(8,128)S(1)}, f32[3,96,128]{2,1,0:T(8,128)S(1)}, f32[6,96,2048]{2,1,0:T(8,128)S(1)}) custom-call(s32[1]{0:T(128)} %bitcast.rep_ref, f32[1,96,12288]{2,1,0:T(8,128)} %x_hbm.1, s32[96,4,192]{2,1,0:T(4,128)} %bitcast.10, s32[8,96,192]{2,1,0:T(8,128)} %cnt_hbm.1, ...), custom_call_target="tpu_custom_call" | custom-call | bytes 12000000 | tf_op jit(solution)/shard_map/pick_other/pallas_call | solution.py:374
  4.2 3.3 %collective-permute-start = (f32[288,128]{1,0:T(8,128)S(1)}, f32[288,128]{1,0:T(8,128)S(1)}, u32[]{:S(2)}, u32[]{:S(2)}) collective-permute-start(f32[288,128]{1,0:T(8,128)S(1)} %bitcast.9), channel_id=1, source_target_pairs={{0,32},{32,0},{64,96},{96,64},{128,160},{160,128},{192,224},{224,1... | collective-permute-start | bytes 442376 | tf_op jit(solution)/shard_map/ppermute | solution.py:459
  7.6 0.0 copy-done.1
  7.6 1.5 %pick_mine.1.mine_ref = f32[3,96,128]{2,1,0:T(8,128)S(1)} custom-call(s32[1]{0:T(128)} %bitcast.rep_ref, f32[6,96,2048]{2,1,0:T(8,128)S(1)} %get-tuple-element.16.x_ref, s32[6,96,128]{2,1,0:T(8,128)S(1)} %get-tuple-element.17.number_ref.chosen_ref, f32[6,96,128]{2,1,0:T(8,128)S(1)} %get-tuple-element.18.live_ref, bf16[256,256]{1,0:T(8,128)(2,1)S(1)} %copy-done.1), custom_call_target="tpu_custom_call" | custom-call | bytes 6000000 | tf_op jit(solution)/shard_map/pick_mine/pallas_call | solution.py:374
  9.1 0.0 collective-permute-done.refs_1_
  9.1 1.1 %collective-permute-start.1 = (f32[288,128]{1,0:T(8,128)S(1)}, f32[288,128]{1,0:T(8,128)S(1)}, u32[]{:S(2)}, u32[]{:S(2)}) collective-permute-start(f32[288,128]{1,0:T(8,128)S(1)} %chip.1.after_ref.refs_0_), channel_id=1, source_target_pairs={{0,64},{32,224},{64,0},{96,160},{128,192},{160,96},{192,128},{224,... | collective-permute-start | bytes 442376 | tf_op jit(solution)/shard_map/ppermute | solution.py:469
  10.2 0.0 copy-done
  10.2 2.6 %residue_0.1 = (f32[1,96,12288]{2,1,0:T(8,128)}, f32[3,128,128]{2,1,0:T(8,128)}, f32[8,128]{1,0:T(8,128)S(1)}) custom-call(s32[1]{0:T(128)} %bitcast.rep_ref, f32[6,96,2048]{2,1,0:T(8,128)S(1)} %get-tuple-element.16.x_ref, s32[6,96,128]{2,1,0:T(8,128)S(1)} %get-tuple-element.17.number_ref.chosen_ref, f32[3,96,128]{2,1,0:T(8,128)S(1)} %pick_mine.1.mine_ref, ...), custom_call_target="tpu_custom_call" | custom-call | bytes 7500000 | tf_op jit(solution)/shard_map/residue_0/pallas_call | solution.py:374
  12.8 1.6 %collective-permute-done.1.refs_1_ = f32[288,128]{1,0:T(8,128)S(1)} collective-permute-done((f32[288,128]{1,0:T(8,128)S(1)}, f32[288,128]{1,0:T(8,128)S(1)}, u32[]{:S(2)}, u32[]{:S(2)}) %collective-permute-start.1) | collective-permute-done | bytes 147488 | tf_op jit(solution)/shard_map/ppermute | solution.py:469
  14.4 0.1 collective-permute-start.2
  14.5 2.6 %residue_1.1 = (f32[1,96,12288]{2,1,0:T(8,128)}, f32[3,128,128]{2,1,0:T(8,128)}, f32[8,128]{1,0:T(8,128)S(1)}) custom-call(s32[1]{0:T(128)} %bitcast.rep_ref, f32[6,96,2048]{2,1,0:T(8,128)S(1)} %get-tuple-element.16.x_ref, s32[6,96,128]{2,1,0:T(8,128)S(1)} %get-tuple-element.17.number_ref.chosen_ref, ...), custom_call_target="tpu_custom_call", output_to_operand_aliasing={{0}: (7, {})} | custom-call | bytes 7500000 | tf_op jit(solution)/shard_map/residue_1/pallas_call | solution.py:374
  17.1 1.4 %collective-permute-done.2.refs_1_ = f32[288,128]{1,0:T(8,128)S(1)} collective-permute-done((f32[288,128]{1,0:T(8,128)S(1)}, f32[288,128]{1,0:T(8,128)S(1)}, u32[]{:S(2)}, u32[]{:S(2)}) %collective-permute-start.2) | collective-permute-done | bytes 147488 | tf_op jit(solution)/shard_map/ppermute | solution.py:469
  18.5 2.4 %collective-permute-start.3 = (f32[288,128]{1,0:T(8,128)S(1)}, f32[288,128]{1,0:T(8,128)S(1)}, u32[]{:S(2)}, u32[]{:S(2)}) collective-permute-start(f32[288,128]{1,0:T(8,128)S(1)} %sum_1.1.a_ref), channel_id=1, source_target_pairs={{0,32},{32,0},{64,96},{96,64},{128,160},{160,128},{192,224},{224,1... | collective-permute-start | bytes 442376 | tf_op jit(solution)/shard_map/ppermute | solution.py:503
  20.9 1.0 %collective-permute-done.3.b_ref = f32[288,128]{1,0:T(8,128)S(1)} collective-permute-done((f32[288,128]{1,0:T(8,128)S(1)}, f32[288,128]{1,0:T(8,128)S(1)}, u32[]{:S(2)}, u32[]{:S(2)}) %collective-permute-start.3) | collective-permute-done | bytes 147488 | tf_op jit(solution)/shard_map/ppermute | solution.py:503
  21.9 0.7 %energy.1 = (f32[32,1,128]{2,1,0:T(1,128)}, f32[8,128]{1,0:T(8,128)S(1)}) custom-call(f32[288,128]{1,0:T(8,128)S(1)} %sum_1.1.a_ref, f32[288,128]{1,0:T(8,128)S(1)} %collective-permute-done.3.b_ref), custom_call_target="tpu_custom_call" | custom-call | bytes 1500000 | tf_op jit(solution)/shard_map/energy/pallas_call | solution.py:374
  22.7 9.3 %all-to-all-start = ((f32[32,1,128]{2,1,0:T(1,128)}), f32[32,1,128]{2,1,0:T(1,128)S(1)}, u32[]{:S(2)}, u32[]{:S(2)}) async-start(f32[32,1,128]{2,1,0:T(1,128)} %get-tuple-element.29), calls=%async_computation | async-start | bytes 32768 | tf_op jit(solution)/shard_map/all_to_all | solution.py:511
  32.0 5.2 %raw.1 = (f32[4,96,2048]{2,1,0:T(8,128)S(1)}, f32[2,96,2048]{2,1,0:T(8,128)}) custom-call(s32[1]{0:T(128)} %bitcast.rep_ref, f32[3,128,128]{2,1,0:T(8,128)} %get-tuple-element.23.low_flip_hbm, f32[3,128,128]{2,1,0:T(8,128)} %get-tuple-element.24.high_flip_hbm, f32[3,96,128]{2,1,0:T(8,128)S(1)} %bitcast.7, f32[3,96,128]{2,1,0:T(8,128)S(1)} %bitcast.8, ...), custom_call_target="tpu_custom_call" | custom-call | bytes 15000000 | tf_op jit(solution)/shard_map/raw/pallas_call | solution.py:374
  37.2 3.4 %all-to-all-done.energy_ref = f32[32,1,128]{2,1,0:T(1,128)S(1)} async-done(((f32[32,1,128]{2,1,0:T(1,128)}), f32[32,1,128]{2,1,0:T(1,128)S(1)}, u32[]{:S(2)}, u32[]{:S(2)}) %all-to-all-start) | async-done | bytes 16416 | tf_op jit(solution)/shard_map/all_to_all | solution.py:511
  40.6 2.8 %update.1 = bf16[96,12288]{1,0:T(8,128)(2,1)} custom-call(f32[4,96,2048]{2,1,0:T(8,128)S(1)} %get-tuple-element.27.near_ref, f32[2,96,2048]{2,1,0:T(8,128)} %get-tuple-element.28.far_hbm, f32[32,1,128]{2,1,0:T(1,128)S(1)} %all-to-all-done.energy_ref), custom_call_target="tpu_custom_call" | custom-call | bytes 6000000 | tf_op jit(solution)/shard_map/update/pallas_call | solution.py:374
  (3 shorter events, 0.1 us)
Async XLA Ops:
  0.6 6.9 %copy-start.1 = (bf16[256,256]{1,0:T(8,128)(2,1)S(1)}, bf16[256,256]{1,0:T(8,128)(2,1)}, u32[]{:S(2)}) copy-start(bf16[256,256]{1,0:T(8,128)(2,1)} %constant.10.clone.w_hbm.w_ref) | copy-start | bytes 393220
  0.6 9.5 %copy-start = (bf16[256,256]{1,0:T(8,128)(2,1)S(1)}, bf16[256,256]{1,0:T(8,128)(2,1)}, u32[]{:S(2)}) copy-start(bf16[256,256]{1,0:T(8,128)(2,1)} %constant.11.clone.w_ref.w_hbm) | copy-start | bytes 393220
  4.2 4.9 %collective-permute-start = (f32[288,128]{1,0:T(8,128)S(1)}, f32[288,128]{1,0:T(8,128)S(1)}, u32[]{:S(2)}, u32[]{:S(2)}) collective-permute-start(f32[288,128]{1,0:T(8,128)S(1)} %bitcast.9), channel_id=1, source_target_pairs={{0,32},{32,0},{64,96},{96,64},{128,160},{160,128},{192,224},{224,1... | collective-permute-start | bytes 442376 | tf_op jit(solution)/shard_map/ppermute | solution.py:459
  9.1 5.3 %collective-permute-start.1 = (f32[288,128]{1,0:T(8,128)S(1)}, f32[288,128]{1,0:T(8,128)S(1)}, u32[]{:S(2)}, u32[]{:S(2)}) collective-permute-start(f32[288,128]{1,0:T(8,128)S(1)} %chip.1.after_ref.refs_0_), channel_id=1, source_target_pairs={{0,64},{32,224},{64,0},{96,160},{128,192},{160,96},{192,128},{224,... | collective-permute-start | bytes 442376 | tf_op jit(solution)/shard_map/ppermute | solution.py:469
  14.4 4.1 %collective-permute-start.2 = (f32[288,128]{1,0:T(8,128)S(1)}, f32[288,128]{1,0:T(8,128)S(1)}, u32[]{:S(2)}, u32[]{:S(2)}) collective-permute-start(f32[288,128]{1,0:T(8,128)S(1)} %sum_0.1.after_ref.refs_0_), channel_id=1, source_target_pairs={{0,192},{32,96},{64,128},{96,32},{128,64},{160,224},{192,0},{224,1... | collective-permute-start | bytes 442376 | tf_op jit(solution)/shard_map/ppermute | solution.py:469
  18.5 3.4 %collective-permute-start.3 = (f32[288,128]{1,0:T(8,128)S(1)}, f32[288,128]{1,0:T(8,128)S(1)}, u32[]{:S(2)}, u32[]{:S(2)}) collective-permute-start(f32[288,128]{1,0:T(8,128)S(1)} %sum_1.1.a_ref), channel_id=1, source_target_pairs={{0,32},{32,0},{64,96},{96,64},{128,160},{160,128},{192,224},{224,1... | collective-permute-start | bytes 442376 | tf_op jit(solution)/shard_map/ppermute | solution.py:503
  22.7 17.9 %all-to-all-start = ((f32[32,1,128]{2,1,0:T(1,128)}), f32[32,1,128]{2,1,0:T(1,128)S(1)}, u32[]{:S(2)}, u32[]{:S(2)}) async-start(f32[32,1,128]{2,1,0:T(1,128)} %get-tuple-element.29), calls=%async_computation | async-start | bytes 32768 | tf_op jit(solution)/shard_map/all_to_all | solution.py:511

commit v5 on v4

--- a/solution.py
+++ b/solution.py
@@ -8,7 +8,7 @@
 from jax import lax
 from jax.experimental import pallas as pl
 from jax.experimental.pallas import tpu as pltpu
-from jax.sharding import PartitionSpec as P
+from jax.sharding import Mesh, PartitionSpec as P
 
 CH = 64
 KEEP = 4
@@ -19,6 +19,8 @@
 TILES = CELLS // PAIR
 WIDTH = TILES * LANES
 BF = jnp.bfloat16
+REP = ("y", "core")
+FSDP = ("z", "x")
 VMEM_BYTES = 32 << 20
 CHUNKS = 4
 
@@ -284,15 +286,16 @@
         at += out.shape[0]
 
 
-def energy_kernel(replicas, a_ref, b_ref, out_ref, done_ref):
-    square = jnp.square(a_ref[...] / replicas) + jnp.square(b_ref[...] / replicas)
+def energy_kernel(replicas, total_ref, out_ref, total_out_ref):
+    total = total_ref[...]
+    total_out_ref[...] = total
+    square = jnp.square(total / replicas)
     energy = jnp.sum(jnp.sum(square, axis=0, keepdims=True), axis=1, keepdims=True)
     out_ref[...] = jnp.broadcast_to(energy[None], out_ref.shape)
-    done_ref[...] = jnp.broadcast_to(energy, done_ref.shape)
 
 
 def raw_kernel(
-    rep_ref, low_flip_hbm, high_flip_hbm, mine_ref, other_ref, w_hbm, after_ref, near_ref, far_hbm,
+    rep_ref, low_flip_hbm, high_flip_hbm, mine_ref, other_ref, w_hbm, near_ref, far_hbm,
     number_ref, high_ref, low_ref, dense_ref, out_ref, flip_ref, w_ref, sem, in_sem,
 ):
     near = near_ref.shape[0]
@@ -391,9 +394,9 @@
     blocks = width // CH
     groups = width // WIDTH
     half = groups // 2
-    replicas = lax.axis_size("rep")
-    shards = lax.axis_size("fsdp")
-    rep = lax.axis_index("rep").astype(jnp.int32).reshape(1)
+    replicas = lax.axis_size(REP)
+    shards = lax.axis_size(FSDP)
+    rep = lax.axis_index(REP).astype(jnp.int32).reshape(1)
     basis = pair_table()
     forward = jnp.asarray(split_weights(basis.T))
     inverse = jnp.asarray(split_weights(basis))
@@ -456,7 +459,7 @@
             )
         )
 
-    partner = lax.ppermute(other.reshape(flat), "rep", swap)
+    partner = lax.ppermute(other.reshape(flat), REP, swap)
     total = add("chip", [mine.reshape(flat)], [partner], [], [piece] * pieces)
     new_moment = None
     flips = []
@@ -464,9 +467,9 @@
         pairs = []
         for y in range(replicas // 2):
             for core in range(2):
-                there = y ^ 1 if part == core else (y + (1 if y % 2 else -1)) % (replicas // 2)
+                there = y ^ 1 if part != core else (y + (1 if y % 2 else -1)) % (replicas // 2)
                 pairs.append((2 * y + core, 2 * there + core))
-        arrived = [lax.ppermute(some, "rep", pairs) for some in total]
+        arrived = [lax.ppermute(some, REP, pairs) for some in total]
         earlier = [] if new_moment is None else [(hbm, new_moment)]
         new_moment, flipped, done = call(
             functools.partial(residue_kernel, part * half),
@@ -500,15 +503,15 @@
         out = [vmem(flat, jnp.float32)] if part else [piece] * pieces
         total = add(f"sum_{part}", total, arrived, [done], out)
     (total,) = total
-    total_other = lax.ppermute(total, "rep", swap)
-    own_energy, summed = call(
+    own_energy, total = call(
         functools.partial(energy_kernel, replicas),
         "energy",
-        [(vmem, total), (vmem, total_other)],
-        [vmem((shards, 1, LANES), jnp.float32), vmem((8, LANES), jnp.float32)],
+        [(vmem, total)],
+        [vmem((2 * shards, 1, LANES), jnp.float32), vmem(flat, jnp.float32)],
         microseconds=0.5,
     )
-    energies = lax.all_to_all(own_energy, "fsdp", 0, 0, tiled=True)
+    energies = lax.all_to_all(own_energy, ("core",) + FSDP, 0, 0, tiled=True)
+    total_other = lax.ppermute(total, REP, swap)
     near = groups * 2 // 3
     far = groups - near
     near_raw, far_raw = call(
@@ -521,7 +524,6 @@
             (vmem, total.reshape(half_shape)),
             (vmem, total_other.reshape(half_shape)),
             (hbm, inverse),
-            (vmem, summed),
         ],
         [vmem((near, rows, WIDTH), jnp.float32), hbm((far, rows, WIDTH), jnp.float32)],
         turned
@@ -546,11 +548,17 @@
 
 
 def solution(mesh):
-    placed = (P("rep", "fsdp", None), P("fsdp", None, None), P(None, "fsdp", None))
+    cores = 2
+    chips = mesh.shape["rep"] // cores
+    lines = 4
+    split = Mesh(
+        mesh.devices.reshape(chips, cores, mesh.shape["fsdp"] // lines, lines), REP + FSDP
+    )
+    placed = (P(REP, FSDP, None), P(FSDP, None, None), P(None, FSDP, None))
     return jax.shard_map(
         per_device,
-        mesh=mesh,
+        mesh=split,
         in_specs=placed,
-        out_specs=(P("rep", "fsdp", None), P("fsdp", None)),
+        out_specs=(P(REP, FSDP, None), P(FSDP, None)),
         check_vma=False,
     )

time: 43.9 us -> 43.9 us (level)
  starting transfers between devices: 16.2 us -> 16.8 us
  waiting for transfers between devices: 7.36 us -> 6.84 us
    ppermute x4, waiting for transfers between devices: 3.97 us -> 2.96 us  [the longest x2 2.95 us: per_device(): arrived = [lax.ppermute(some, REP, pairs) for some in total]]
    all_to_all x1, starting transfers between devices: 9.3 us -> 9.97 us  [per_device(): energies = lax.all_to_all(own_energy, ('core',) + FSDP, 0, 0, tiled=True)]
    all_to_all x1, waiting for transfers between devices: 3.39 us -> 3.88 us  [per_device(): energies = lax.all_to_all(own_energy, ('core',) + FSDP, 0, 0, tiled=True)]
  transfers between devices with their start and end apart: 5 -> 5, of which waited for: 4 -> 3; matrix products, arithmetic and copies ran while one was open for 0% -> 0% of each run, Pallas kernels for 27% -> 27%
where the time goes in v5:
time: 43.9 us; the launch traced here: 43.6 us
  Pallas kernels  19.1 us (44%)
  starting transfers between devices  16.8 us (38%)
  waiting for transfers between devices  6.84 us (16%)
  between operations  0.91 us (2%)
    pallas_call x10, Pallas kernels, call(): pl.pallas_call(kernel, in_specs=specs, out_specs=outs if isinstance(out_s...  19.1 us
    all_to_all x1, starting transfers between devices, per_device(): energies = lax.all_to_all(own_energy, ('core',) + FSDP, 0, 0, tiled=True)  9.97 us
    all_to_all x1, waiting for transfers between devices, per_device(): energies = lax.all_to_all(own_energy, ('core',) + FSDP, 0, 0, tiled=True)  3.88 us
    ppermute x1, starting transfers between devices, per_device(): partner = lax.ppermute(other.reshape(flat), REP, swap)  3.33 us
    ppermute x2, waiting for transfers between devices, per_device(): arrived = [lax.ppermute(some, REP, pairs) for some in total]  2.95 us
    ppermute x1, starting transfers between devices, per_device(): total_other = lax.ppermute(total, REP, swap)  2.32 us
    ppermute x2, starting transfers between devices, per_device(): arrived = [lax.ppermute(some, REP, pairs) for some in total]  1.18 us
  transfers between devices with their start and end apart: 5, of which 3 were waited for; matrix products, arithmetic and copies ran while one was open for 0% of the time, Pallas kernels for 27%

profile of v5, /device:TPU:1, one launch (start us, length us, event | category | flops | bytes accessed | tf_op | source)
XLA Modules:
  0.0 43.6 jit_solution(14138333317788027836)
XLA Ops:
  0.6 0.0 copy-start.1
  0.6 0.0 copy-start
  0.7 3.6 %pick_other.1 = (s32[6,96,128]{2,1,0:T(8,128)S(1)}, f32[6,96,128]{2,1,0:T(8,128)S(1)}, f32[3,96,128]{2,1,0:T(8,128)S(1)}, f32[6,96,2048]{2,1,0:T(8,128)S(1)}) custom-call(s32[1]{0:T(128)} %bitcast.rep_ref, f32[1,96,12288]{2,1,0:T(8,128)} %x_hbm.1, s32[96,4,192]{2,1,0:T(4,128)} %bitcast.10, s32[8,96,192]{2,1,0:T(8,128)} %cnt_hbm.1, ...), custom_call_target="tpu_custom_call" | custom-call | bytes 12000000 | tf_op jit(solution)/shard_map/pick_other/pallas_call | solution.py:377
  4.2 3.3 %collective-permute-start = (f32[288,128]{1,0:T(8,128)S(1)}, f32[288,128]{1,0:T(8,128)S(1)}, u32[]{:S(2)}, u32[]{:S(2)}) collective-permute-start(f32[288,128]{1,0:T(8,128)S(1)} %bitcast.7), channel_id=1, source_target_pairs={{0,32},{32,0},{64,96},{96,64},{128,160},{160,128},{192,224},{224,1... | collective-permute-start | bytes 442376 | tf_op jit(solution)/shard_map/ppermute | solution.py:462
  7.6 0.0 copy-done.1
  7.6 1.5 %pick_mine.1.mine_ref = f32[3,96,128]{2,1,0:T(8,128)S(1)} custom-call(s32[1]{0:T(128)} %bitcast.rep_ref, f32[6,96,2048]{2,1,0:T(8,128)S(1)} %get-tuple-element.16.x_ref, s32[6,96,128]{2,1,0:T(8,128)S(1)} %get-tuple-element.17.number_ref.chosen_ref, f32[6,96,128]{2,1,0:T(8,128)S(1)} %get-tuple-element.18.live_ref, bf16[256,256]{1,0:T(8,128)(2,1)S(1)} %copy-done.1), custom_call_target="tpu_custom_call" | custom-call | bytes 6000000 | tf_op jit(solution)/shard_map/pick_mine/pallas_call | solution.py:377
  9.1 0.0 collective-permute-done.refs_1_
  9.1 0.1 collective-permute-start.1
  9.2 0.0 copy-done
  9.2 2.6 %residue_0.1 = (f32[1,96,12288]{2,1,0:T(8,128)}, f32[3,128,128]{2,1,0:T(8,128)}, f32[8,128]{1,0:T(8,128)S(1)}) custom-call(s32[1]{0:T(128)} %bitcast.rep_ref, f32[6,96,2048]{2,1,0:T(8,128)S(1)} %get-tuple-element.16.x_ref, s32[6,96,128]{2,1,0:T(8,128)S(1)} %get-tuple-element.17.number_ref.chosen_ref, f32[3,96,128]{2,1,0:T(8,128)S(1)} %pick_mine.1.mine_ref, ...), custom_call_target="tpu_custom_call" | custom-call | bytes 7500000 | tf_op jit(solution)/shard_map/residue_0/pallas_call | solution.py:377
  11.8 1.4 %collective-permute-done.1.refs_1_ = f32[288,128]{1,0:T(8,128)S(1)} collective-permute-done((f32[288,128]{1,0:T(8,128)S(1)}, f32[288,128]{1,0:T(8,128)S(1)}, u32[]{:S(2)}, u32[]{:S(2)}) %collective-permute-start.1) | collective-permute-done | bytes 147488 | tf_op jit(solution)/shard_map/ppermute | solution.py:472
  13.2 1.1 %collective-permute-start.2 = (f32[288,128]{1,0:T(8,128)S(1)}, f32[288,128]{1,0:T(8,128)S(1)}, u32[]{:S(2)}, u32[]{:S(2)}) collective-permute-start(f32[288,128]{1,0:T(8,128)S(1)} %sum_0.1.after_ref.refs_0_), channel_id=1, source_target_pairs={{0,64},{32,224},{64,0},{96,160},{128,192},{160,96},{192,128},{224,... | collective-permute-start | bytes 442376 | tf_op jit(solution)/shard_map/ppermute | solution.py:472
  14.3 2.6 %residue_1.1 = (f32[1,96,12288]{2,1,0:T(8,128)}, f32[3,128,128]{2,1,0:T(8,128)}, f32[8,128]{1,0:T(8,128)S(1)}) custom-call(s32[1]{0:T(128)} %bitcast.rep_ref, f32[6,96,2048]{2,1,0:T(8,128)S(1)} %get-tuple-element.16.x_ref, s32[6,96,128]{2,1,0:T(8,128)S(1)} %get-tuple-element.17.number_ref.chosen_ref, ...), custom_call_target="tpu_custom_call", output_to_operand_aliasing={{0}: (7, {})} | custom-call | bytes 7500000 | tf_op jit(solution)/shard_map/residue_1/pallas_call | solution.py:377
  16.9 1.6 %collective-permute-done.2.refs_1_ = f32[288,128]{1,0:T(8,128)S(1)} collective-permute-done((f32[288,128]{1,0:T(8,128)S(1)}, f32[288,128]{1,0:T(8,128)S(1)}, u32[]{:S(2)}, u32[]{:S(2)}) %collective-permute-start.2) | collective-permute-done | bytes 147488 | tf_op jit(solution)/shard_map/ppermute | solution.py:472
  18.5 0.8 %energy.1 = (f32[64,1,128]{2,1,0:T(1,128)}, f32[288,128]{1,0:T(8,128)S(1)}) custom-call(f32[288,128]{1,0:T(8,128)S(1)} %sum_1.1.total_ref), custom_call_target="tpu_custom_call" | custom-call | bytes 1500000 | tf_op jit(solution)/shard_map/energy/pallas_call | solution.py:377
  19.3 2.3 %collective-permute-start.3 = (f32[288,128]{1,0:T(8,128)S(1)}, f32[288,128]{1,0:T(8,128)S(1)}, u32[]{:S(2)}, u32[]{:S(2)}) collective-permute-start(f32[288,128]{1,0:T(8,128)S(1)} %get-tuple-element.26), channel_id=1, source_target_pairs={{0,32},{32,0},{64,96},{96,64},{128,160},{160,128},{192,224},{224,1... | collective-permute-start | bytes 442376 | tf_op jit(solution)/shard_map/ppermute | solution.py:514
  21.6 10.0 %all-to-all-start = ((f32[64,1,128]{2,1,0:T(1,128)}), f32[64,1,128]{2,1,0:T(1,128)S(1)}, u32[]{:S(2)}, u32[]{:S(2)}) async-start(f32[64,1,128]{2,1,0:T(1,128)} %get-tuple-element.29), calls=%async_computation | async-start | bytes 65536 | tf_op jit(solution)/shard_map/all_to_all | solution.py:513
  31.6 0.0 collective-permute-done.3
  31.6 5.2 %raw.1 = (f32[4,96,2048]{2,1,0:T(8,128)S(1)}, f32[2,96,2048]{2,1,0:T(8,128)}) custom-call(s32[1]{0:T(128)} %bitcast.rep_ref, f32[3,128,128]{2,1,0:T(8,128)} %get-tuple-element.23.low_flip_hbm, f32[3,128,128]{2,1,0:T(8,128)} %get-tuple-element.24.high_flip_hbm, f32[3,96,128]{2,1,0:T(8,128)S(1)} %bitcast.8, f32[3,96,128]{2,1,0:T(8,128)S(1)} %bitcast.9, ...), custom_call_target="tpu_custom_call" | custom-call | bytes 15000000 | tf_op jit(solution)/shard_map/raw/pallas_call | solution.py:377
  36.8 3.9 %all-to-all-done.energy_ref = f32[64,1,128]{2,1,0:T(1,128)S(1)} async-done(((f32[64,1,128]{2,1,0:T(1,128)}), f32[64,1,128]{2,1,0:T(1,128)S(1)}, u32[]{:S(2)}, u32[]{:S(2)}) %all-to-all-start) | async-done | bytes 32800 | tf_op jit(solution)/shard_map/all_to_all | solution.py:513
  40.7 2.8 %update.1 = bf16[96,12288]{1,0:T(8,128)(2,1)} custom-call(f32[4,96,2048]{2,1,0:T(8,128)S(1)} %get-tuple-element.27.near_ref, f32[2,96,2048]{2,1,0:T(8,128)} %get-tuple-element.28.far_hbm, f32[64,1,128]{2,1,0:T(1,128)S(1)} %all-to-all-done.energy_ref), custom_call_target="tpu_custom_call" | custom-call | bytes 6000000 | tf_op jit(solution)/shard_map/update/pallas_call | solution.py:377
  (3 shorter events, 0.1 us)
Async XLA Ops:
  0.6 6.9 %copy-start.1 = (bf16[256,256]{1,0:T(8,128)(2,1)S(1)}, bf16[256,256]{1,0:T(8,128)(2,1)}, u32[]{:S(2)}) copy-start(bf16[256,256]{1,0:T(8,128)(2,1)} %constant.18.clone.w_hbm.w_ref) | copy-start | bytes 393220
  0.6 8.6 %copy-start = (bf16[256,256]{1,0:T(8,128)(2,1)S(1)}, bf16[256,256]{1,0:T(8,128)(2,1)}, u32[]{:S(2)}) copy-start(bf16[256,256]{1,0:T(8,128)(2,1)} %constant.19.clone.w_ref.w_hbm) | copy-start | bytes 393220
  4.2 4.8 %collective-permute-start = (f32[288,128]{1,0:T(8,128)S(1)}, f32[288,128]{1,0:T(8,128)S(1)}, u32[]{:S(2)}, u32[]{:S(2)}) collective-permute-start(f32[288,128]{1,0:T(8,128)S(1)} %bitcast.7), channel_id=1, source_target_pairs={{0,32},{32,0},{64,96},{96,64},{128,160},{160,128},{192,224},{224,1... | collective-permute-start | bytes 442376 | tf_op jit(solution)/shard_map/ppermute | solution.py:462
  9.1 4.1 %collective-permute-start.1 = (f32[288,128]{1,0:T(8,128)S(1)}, f32[288,128]{1,0:T(8,128)S(1)}, u32[]{:S(2)}, u32[]{:S(2)}) collective-permute-start(f32[288,128]{1,0:T(8,128)S(1)} %chip.1.after_ref.refs_0_), channel_id=1, source_target_pairs={{0,192},{32,96},{64,128},{96,32},{128,64},{160,224},{192,0},{224,1... | collective-permute-start | bytes 442376 | tf_op jit(solution)/shard_map/ppermute | solution.py:472
  13.2 5.3 %collective-permute-start.2 = (f32[288,128]{1,0:T(8,128)S(1)}, f32[288,128]{1,0:T(8,128)S(1)}, u32[]{:S(2)}, u32[]{:S(2)}) collective-permute-start(f32[288,128]{1,0:T(8,128)S(1)} %sum_0.1.after_ref.refs_0_), channel_id=1, source_target_pairs={{0,64},{32,224},{64,0},{96,160},{128,192},{160,96},{192,128},{224,... | collective-permute-start | bytes 442376 | tf_op jit(solution)/shard_map/ppermute | solution.py:472
  19.3 12.3 %collective-permute-start.3 = (f32[288,128]{1,0:T(8,128)S(1)}, f32[288,128]{1,0:T(8,128)S(1)}, u32[]{:S(2)}, u32[]{:S(2)}) collective-permute-start(f32[288,128]{1,0:T(8,128)S(1)} %get-tuple-element.26), channel_id=1, source_target_pairs={{0,32},{32,0},{64,96},{96,64},{128,160},{160,128},{192,224},{224,1... | collective-permute-start | bytes 442376 | tf_op jit(solution)/shard_map/ppermute | solution.py:514
  21.6 19.1 %all-to-all-start = ((f32[64,1,128]{2,1,0:T(1,128)}), f32[64,1,128]{2,1,0:T(1,128)S(1)}, u32[]{:S(2)}, u32[]{:S(2)}) async-start(f32[64,1,128]{2,1,0:T(1,128)} %get-tuple-element.29), calls=%async_computation | async-start | bytes 65536 | tf_op jit(solution)/shard_map/all_to_all | solution.py:513

commit v6 on v5

--- a/solution.py
+++ b/solution.py
@@ -250,7 +250,7 @@
         return pltpu.make_async_copy(out_ref.at[i], out_hbm.at[0, :, columns(first + i)], sem.at[i])
 
     def flip_copy(i):
-        return pltpu.make_async_copy(flip_ref.at[i], flip_hbm.at[i], flip_sem.at[i])
+        return pltpu.make_async_copy(flip_ref.at[i], flip_hbm.at[first + i], flip_sem.at[i])
 
     def numbers_of(i):
         turned = flip(chosen_ref[first + i].astype(jnp.float32))
@@ -286,92 +286,83 @@
         at += out.shape[0]
 
 
-def energy_kernel(replicas, total_ref, out_ref, total_out_ref):
+def energy_kernel(replicas, total_ref, out_ref, total_out_ref, saved_ref):
     total = total_ref[...]
     total_out_ref[...] = total
+    saved_ref[...] = total
     square = jnp.square(total / replicas)
     energy = jnp.sum(jnp.sum(square, axis=0, keepdims=True), axis=1, keepdims=True)
     out_ref[...] = jnp.broadcast_to(energy[None], out_ref.shape)
 
 
 def raw_kernel(
-    rep_ref, low_flip_hbm, high_flip_hbm, mine_ref, other_ref, w_hbm, near_ref, far_hbm,
-    number_ref, high_ref, low_ref, dense_ref, out_ref, flip_ref, w_ref, sem, in_sem,
+    rep_ref, flip_hbm, mine_hbm, other_hbm, w_hbm, near_ref, value_out_ref, flip_out_ref, w_ref,
+    number_ref, high_ref, low_ref, dense_ref, flip_ref, mine_ref, other_ref, sem,
 ):
-    near = near_ref.shape[0]
-    groups = near + out_ref.shape[0]
+    near, far = near_ref.shape[0], flip_out_ref.shape[0]
     fetches = [
-        pltpu.make_async_copy(low_flip_hbm, flip_ref.at[: groups // 2], in_sem.at[0]),
-        pltpu.make_async_copy(high_flip_hbm, flip_ref.at[groups // 2 :], in_sem.at[1]),
-        pltpu.make_async_copy(w_hbm, w_ref, in_sem.at[2]),
+        pltpu.make_async_copy(flip_hbm.at[:near], flip_ref, sem.at[0]),
+        pltpu.make_async_copy(flip_hbm.at[near:], flip_out_ref, sem.at[1]),
+        pltpu.make_async_copy(mine_hbm, mine_ref, sem.at[2]),
+        pltpu.make_async_copy(other_hbm, other_ref, sem.at[3]),
+        pltpu.make_async_copy(w_hbm, w_ref, sem.at[4]),
     ]
     for fetch in fetches:
         fetch.start()
     for fetch in fetches:
         fetch.wait()
 
-    def copy(i):
-        return pltpu.make_async_copy(out_ref.at[i], far_hbm.at[i], sem.at[i])
-
     def store(g, t, part):
-        far = groups - 1 - g
-        if t is None:
-            copy(far).start() if g >= near else None
-        elif g >= near:
-            out_ref[far, :, t * LANES : (t + 1) * LANES] = part
-        else:
+        if t is not None:
             near_ref[g, :, t * LANES : (t + 1) * LANES] = part
 
     decode(
-        groups, lambda g: flip_ref[g], lambda g: side(rep_ref, mine_ref, other_ref, g), w_ref,
+        near, lambda g: flip_ref[g], lambda g: side(rep_ref, mine_ref, other_ref, g), w_ref,
         number_ref, high_ref, low_ref, dense_ref, store, True,
     )
-    for i in range(groups - near):
-        copy(i).wait()
-
-
-def update_kernel(entries, replicas, near_ref, far_hbm, energy_ref, out_hbm, far_ref, out_ref, far_sem, sem):
+    for i in range(far):
+        value_out_ref[i] = side(rep_ref, mine_ref, other_ref, near + i)
+
+
+def update_kernel(
+    entries, replicas, near_ref, value_ref, flip_ref, w_ref, energy_ref, out_hbm,
+    number_ref, high_ref, low_ref, dense_ref, out_ref, sem,
+):
     groups = out_ref.shape[0]
     near = near_ref.shape[0]
-
-    def fetch(i):
-        return pltpu.make_async_copy(far_hbm.at[i], far_ref.at[i], far_sem.at[i])
+    energy = jnp.sum(energy_ref[:, 0, :], axis=0, keepdims=True)
+    scale = lax.rsqrt(energy / entries + 1e-06) / replicas
+    wide = jnp.concatenate([scale] * TILES, axis=1)
 
     def copy(g):
         return pltpu.make_async_copy(out_ref.at[g], out_hbm.at[:, columns(g)], sem.at[g])
 
-    for i in range(groups - near):
-        fetch(i).start()
-    energy = jnp.sum(energy_ref[:, 0, :], axis=0, keepdims=True)
-    scale = lax.rsqrt(energy / entries + 1e-06) / replicas
-    scale = jnp.concatenate([scale] * TILES, axis=1)
-
-    def near_body(g, carry):
-        out_ref[g] = (near_ref[g] * scale).astype(BF)
+    for g in range(near):
+        out_ref[g] = (near_ref[g] * wide).astype(BF)
         copy(g).start()
-        return carry
-
-    def far_body(i, carry):
-        fetch(i).wait()
-        g = groups - 1 - i
-        out_ref[g] = (far_ref[i] * scale).astype(BF)
-        copy(g).start()
-        return carry
-
-    lax.fori_loop(0, near, near_body, 0)
-    lax.fori_loop(0, groups - near, far_body, 0)
+
+    def store(i, t, part):
+        if t is None:
+            copy(near + i).start()
+        else:
+            out_ref[near + i, :, t * LANES : (t + 1) * LANES] = part.astype(BF)
+
+    decode(
+        groups - near, lambda i: flip_ref[i], lambda i: value_ref[i] * scale, w_ref,
+        number_ref, high_ref, low_ref, dense_ref, store, True,
+    )
     for g in range(groups):
         copy(g).wait()
 
 
-def call(kernel, name, operands, out_shape, scratch=(), microseconds=1.0, aliases=()):
+def call(kernel, name, operands, out_shape, scratch=(), microseconds=1.0, aliases=(), blocked=False):
     specs, arrays = [], []
     for place, array in operands:
         specs.append(pl.BlockSpec(memory_space=place))
         arrays.append(pltpu.with_memory_space_constraint(array, place) if place is pltpu.HBM else array)
     shapes = out_shape if isinstance(out_shape, list) else [out_shape]
     outs = [
-        pl.BlockSpec(memory_space=pltpu.HBM if shape.memory_space is pltpu.HBM else pltpu.VMEM)
+        pl.BlockSpec(memory_space=pltpu.HBM if shape.memory_space is pltpu.HBM and not blocked else pltpu.VMEM)
         for shape in shapes
     ]
     return pl.pallas_call(
@@ -462,7 +453,6 @@
     partner = lax.ppermute(other.reshape(flat), REP, swap)
     total = add("chip", [mine.reshape(flat)], [partner], [], [piece] * pieces)
     new_moment = None
-    flips = []
     for part in range(2):
         pairs = []
         for y in range(replicas // 2):
@@ -470,8 +460,8 @@
                 there = y ^ 1 if part != core else (y + (1 if y % 2 else -1)) % (replicas // 2)
                 pairs.append((2 * y + core, 2 * there + core))
         arrived = [lax.ppermute(some, REP, pairs) for some in total]
-        earlier = [] if new_moment is None else [(hbm, new_moment)]
-        new_moment, flipped, done = call(
+        earlier = [] if new_moment is None else [(hbm, new_moment), (hbm, flips)]
+        new_moment, flips, done = call(
             functools.partial(residue_kernel, part * half),
             f"residue_{part}",
             [
@@ -486,7 +476,7 @@
             + earlier,
             [
                 hbm(momentum.shape, jnp.float32),
-                hbm((half, LANES, LANES), jnp.float32),
+                hbm((groups, LANES, LANES), jnp.float32),
                 vmem((8, LANES), jnp.float32),
             ],
             turned
@@ -497,51 +487,54 @@
                 dma((half,)),
             ],
             2.5,
-            {7: 0} if earlier else {},
+            {7: 0, 8: 1} if earlier else {},
         )
-        flips.append(flipped)
         out = [vmem(flat, jnp.float32)] if part else [piece] * pieces
         total = add(f"sum_{part}", total, arrived, [done], out)
     (total,) = total
-    own_energy, total = call(
+    own_energy, total, saved = call(
         functools.partial(energy_kernel, replicas),
         "energy",
         [(vmem, total)],
-        [vmem((2 * shards, 1, LANES), jnp.float32), vmem(flat, jnp.float32)],
+        [vmem((2 * shards, 1, LANES), jnp.float32), vmem(flat, jnp.float32), hbm(flat, jnp.float32)],
         microseconds=0.5,
+        blocked=True,
     )
     energies = lax.all_to_all(own_energy, ("core",) + FSDP, 0, 0, tiled=True)
     total_other = lax.ppermute(total, REP, swap)
     near = groups * 2 // 3
     far = groups - near
-    near_raw, far_raw = call(
+    raw, values, turns, weights = call(
         raw_kernel,
         "raw",
         [
             (smem, rep),
-            (hbm, flips[0]),
-            (hbm, flips[1]),
-            (vmem, total.reshape(half_shape)),
-            (vmem, total_other.reshape(half_shape)),
+            (hbm, flips),
+            (hbm, saved.reshape(half_shape)),
+            (hbm, total_other.reshape(half_shape)),
             (hbm, inverse),
         ],
-        [vmem((near, rows, WIDTH), jnp.float32), hbm((far, rows, WIDTH), jnp.float32)],
+        [
+            vmem((near, rows, WIDTH), jnp.float32),
+            vmem((far, rows, LANES), jnp.float32),
+            vmem((far, LANES, LANES), jnp.float32),
+            vmem(inverse.shape, BF),
+        ],
         turned
         + [
-            vmem((far, rows, WIDTH), jnp.float32),
-            vmem((groups, LANES, LANES), jnp.float32),
-            vmem(inverse.shape, BF),
-            dma((far,)),
-            dma((3,)),
+            vmem((near, LANES, LANES), jnp.float32),
+            vmem(half_shape, jnp.float32),
+            vmem(half_shape, jnp.float32),
+            dma((5,)),
         ],
         5.0,
     )
     update = call(
         functools.partial(update_kernel, rows * width * shards, replicas),
         "update",
-        [(vmem, near_raw), (hbm, far_raw), (vmem, energies)],
+        [(vmem, raw), (vmem, values), (vmem, turns), (vmem, weights), (vmem, energies)],
         hbm((rows, width), BF),
-        [vmem((far, rows, WIDTH), jnp.float32), vmem((groups, rows, WIDTH), BF), dma((far,)), dma((groups,))],
+        turned + [vmem((groups, rows, WIDTH), BF), dma((groups,))],
         2.0,
     )
     return new_moment, update

time: 43.9 us -> 43.3 us (0.986)
  Pallas kernels: 19.1 us -> 16.7 us
  waiting for transfers between devices: 6.84 us -> 8.03 us
  local copies, waits for them, and re-layouts: 0.01 us -> 0.67 us
    pallas_call x10, Pallas kernels: 19.1 us -> 16.7 us  [call(): pl.pallas_call(kernel, in_specs=specs, out_specs=outs if isinstance(out_s...]
    all_to_all x1, waiting for transfers between devices: 3.88 us -> 5.06 us  [per_device(): energies = lax.all_to_all(own_energy, ('core',) + FSDP, 0, 0, tiled=True)]
    unnamed x4 -> x6, local copies, waits for them, and re-layouts: 0.01 us -> 0.67 us
  transfers between devices with their start and end apart: 5 -> 5, of which waited for: 3 -> 3; matrix products, arithmetic and copies ran while one was open for 0% -> 0% of each run, Pallas kernels for 27% -> 23%
where the time goes in v6:
time: 43.3 us; the launch traced here: 43.1 us
  starting transfers between devices  16.8 us (39%)
  Pallas kernels  16.7 us (39%)
  waiting for transfers between devices  8.03 us (19%)
  between operations  0.92 us (2%)
  local copies, waits for them, and re-layouts  0.67 us (2%)
    pallas_call x10, Pallas kernels, call(): pl.pallas_call(kernel, in_specs=specs, out_specs=outs if isinstance(out_s...  16.7 us
    all_to_all x1, starting transfers between devices, per_device(): energies = lax.all_to_all(own_energy, ('core',) + FSDP, 0, 0, tiled=True)  9.97 us
    all_to_all x1, waiting for transfers between devices, per_device(): energies = lax.all_to_all(own_energy, ('core',) + FSDP, 0, 0, tiled=True)  5.06 us
    ppermute x1, starting transfers between devices, per_device(): partner = lax.ppermute(other.reshape(flat), REP, swap)  3.33 us
    ppermute x2, waiting for transfers between devices, per_device(): arrived = [lax.ppermute(some, REP, pairs) for some in total]  2.96 us
    ppermute x1, starting transfers between devices, per_device(): total_other = lax.ppermute(total, REP, swap)  2.32 us
    ppermute x2, starting transfers between devices, per_device(): arrived = [lax.ppermute(some, REP, pairs) for some in total]  1.18 us
  transfers between devices with their start and end apart: 5, of which 3 were waited for; matrix products, arithmetic and copies ran while one was open for 0% of the time, Pallas kernels for 23%

profile of v6, /device:TPU:1, one launch (start us, length us, event | category | flops | bytes accessed | tf_op | source)
XLA Modules:
  0.0 43.1 jit_solution(17654229795047156091)
XLA Ops:
  0.6 0.0 copy-start.1
  0.6 0.0 copy-start
  0.7 3.6 %pick_other.1 = (s32[6,96,128]{2,1,0:T(8,128)S(1)}, f32[6,96,128]{2,1,0:T(8,128)S(1)}, f32[3,96,128]{2,1,0:T(8,128)S(1)}, f32[6,96,2048]{2,1,0:T(8,128)S(1)}) custom-call(s32[1]{0:T(128)} %bitcast.rep_ref, f32[1,96,12288]{2,1,0:T(8,128)} %x_hbm.1, s32[96,4,192]{2,1,0:T(4,128)} %bitcast.8, s32[8,96,192]{2,1,0:T(8,128)} %cnt_hbm.1, ...), custom_call_target="tpu_custom_call" | custom-call | bytes 12000000 | tf_op jit(solution)/shard_map/pick_other/pallas_call | solution.py:368
  4.2 3.3 %collective-permute-start = (f32[288,128]{1,0:T(8,128)S(1)}, f32[288,128]{1,0:T(8,128)S(1)}, u32[]{:S(2)}, u32[]{:S(2)}) collective-permute-start(f32[288,128]{1,0:T(8,128)S(1)} %bitcast.7), channel_id=1, source_target_pairs={{0,32},{32,0},{64,96},{96,64},{128,160},{160,128},{192,224},{224,1... | collective-permute-start | bytes 442376 | tf_op jit(solution)/shard_map/ppermute | solution.py:453
  7.6 0.0 copy-done.1
  7.6 1.5 %pick_mine.1.mine_ref = f32[3,96,128]{2,1,0:T(8,128)S(1)} custom-call(s32[1]{0:T(128)} %bitcast.rep_ref, f32[6,96,2048]{2,1,0:T(8,128)S(1)} %get-tuple-element.19.x_ref, s32[6,96,128]{2,1,0:T(8,128)S(1)} %get-tuple-element.20.number_ref.chosen_ref, f32[6,96,128]{2,1,0:T(8,128)S(1)} %get-tuple-element.21.live_ref, bf16[256,256]{1,0:T(8,128)(2,1)S(1)} %copy-done.1), custom_call_target="tpu_custom_call" | custom-call | bytes 6000000 | tf_op jit(solution)/shard_map/pick_mine/pallas_call | solution.py:368
  9.1 0.0 collective-permute-done.refs_1_
  9.1 0.1 collective-permute-start.1
  9.2 0.0 copy-done
  9.2 2.6 %residue_0.1 = (f32[1,96,12288]{2,1,0:T(8,128)}, f32[6,128,128]{2,1,0:T(8,128)}, f32[8,128]{1,0:T(8,128)S(1)}) custom-call(s32[1]{0:T(128)} %bitcast.rep_ref, f32[6,96,2048]{2,1,0:T(8,128)S(1)} %get-tuple-element.19.x_ref, s32[6,96,128]{2,1,0:T(8,128)S(1)} %get-tuple-element.20.number_ref.chosen_ref, f32[3,96,128]{2,1,0:T(8,128)S(1)} %pick_mine.1.mine_ref, ...), custom_call_target="tpu_custom_call" | custom-call | bytes 7500000 | tf_op jit(solution)/shard_map/residue_0/pallas_call | solution.py:368
  11.8 1.4 %collective-permute-done.1.refs_1_ = f32[288,128]{1,0:T(8,128)S(1)} collective-permute-done((f32[288,128]{1,0:T(8,128)S(1)}, f32[288,128]{1,0:T(8,128)S(1)}, u32[]{:S(2)}, u32[]{:S(2)}) %collective-permute-start.1) | collective-permute-done | bytes 147488 | tf_op jit(solution)/shard_map/ppermute | solution.py:462
  13.2 1.1 %collective-permute-start.2 = (f32[288,128]{1,0:T(8,128)S(1)}, f32[288,128]{1,0:T(8,128)S(1)}, u32[]{:S(2)}, u32[]{:S(2)}) collective-permute-start(f32[288,128]{1,0:T(8,128)S(1)} %sum_0.1.after_ref.refs_0_), channel_id=1, source_target_pairs={{0,64},{32,224},{64,0},{96,160},{128,192},{160,96},{192,128},{224,... | collective-permute-start | bytes 442376 | tf_op jit(solution)/shard_map/ppermute | solution.py:462
  14.3 2.6 %residue_1.1 = (f32[1,96,12288]{2,1,0:T(8,128)}, f32[6,128,128]{2,1,0:T(8,128)}, f32[8,128]{1,0:T(8,128)S(1)}) custom-call(s32[1]{0:T(128)} %bitcast.rep_ref, f32[6,96,2048]{2,1,0:T(8,128)S(1)} %get-tuple-element.19.x_ref, s32[6,96,128]{2,1,0:T(8,128)S(1)} %get-tuple-element.20.number_ref.chosen_ref, ...), custom_call_target="tpu_custom_call", output_to_operand_aliasing={{0}: (7, {}), {1}: (8, {})} | custom-call | bytes 7500000 | tf_op jit(solution)/shard_map/residue_1/pallas_call | solution.py:368
  16.9 1.6 %collective-permute-done.2.refs_1_ = f32[288,128]{1,0:T(8,128)S(1)} collective-permute-done((f32[288,128]{1,0:T(8,128)S(1)}, f32[288,128]{1,0:T(8,128)S(1)}, u32[]{:S(2)}, u32[]{:S(2)}) %collective-permute-start.2) | collective-permute-done | bytes 147488 | tf_op jit(solution)/shard_map/ppermute | solution.py:462
  18.5 0.7 %energy.1 = (f32[64,1,128]{2,1,0:T(1,128)}, f32[288,128]{1,0:T(8,128)S(1)}, f32[288,128]{1,0:T(8,128)}) custom-call(f32[288,128]{1,0:T(8,128)S(1)} %sum_1.1.total_ref), custom_call_target="tpu_custom_call" | custom-call | bytes 1500000 | tf_op jit(solution)/shard_map/energy/pallas_call | solution.py:368
  19.3 2.3 %collective-permute-start.3 = (f32[288,128]{1,0:T(8,128)S(1)}, f32[288,128]{1,0:T(8,128)S(1)}, u32[]{:S(2)}, u32[]{:S(2)}) collective-permute-start(f32[288,128]{1,0:T(8,128)S(1)} %get-tuple-element.30), channel_id=1, source_target_pairs={{0,32},{32,0},{64,96},{96,64},{128,160},{160,128},{192,224},{224,1... | collective-permute-start | bytes 442376 | tf_op jit(solution)/shard_map/ppermute | solution.py:504
  21.6 10.0 %all-to-all-start = ((f32[64,1,128]{2,1,0:T(1,128)}), f32[64,1,128]{2,1,0:T(1,128)S(1)}, u32[]{:S(2)}, u32[]{:S(2)}) async-start(f32[64,1,128]{2,1,0:T(1,128)} %get-tuple-element.35), calls=%async_computation | async-start | bytes 65536 | tf_op jit(solution)/shard_map/all_to_all | solution.py:503
  31.6 0.0 collective-permute-done.3
  31.6 0.0 copy-start.2
  31.6 0.7 %copy-done.2 = f32[288,128]{1,0:T(8,128)} copy-done((f32[288,128]{1,0:T(8,128)}, f32[288,128]{1,0:T(8,128)S(1)}, u32[]{:S(2)}) %copy-start.2) | copy-done | bytes 147480
  32.2 3.4 %raw.1 = (f32[4,96,2048]{2,1,0:T(8,128)S(1)}, f32[2,96,128]{2,1,0:T(8,128)S(1)}, f32[2,128,128]{2,1,0:T(8,128)S(1)}, bf16[256,256]{1,0:T(8,128)(2,1)S(1)}) custom-call(s32[1]{0:T(128)} %bitcast.rep_ref, f32[6,128,128]{2,1,0:T(8,128)} %get-tuple-element.27.flip_hbm, f32[3,96,128]{2,1,0:T(8,128)} %bitcast.9, f32[3,96,128]{2,1,0:T(8,128)} %bitcast.10, ...), custom_call_target="tpu_custom_call" | custom-call | bytes 15000000 | tf_op jit(solution)/shard_map/raw/pallas_call | solution.py:368
  35.6 5.1 %all-to-all-done.energy_ref = f32[64,1,128]{2,1,0:T(1,128)S(1)} async-done(((f32[64,1,128]{2,1,0:T(1,128)}), f32[64,1,128]{2,1,0:T(1,128)S(1)}, u32[]{:S(2)}, u32[]{:S(2)}) %all-to-all-start) | async-done | bytes 32800 | tf_op jit(solution)/shard_map/all_to_all | solution.py:503
  40.7 2.3 %update.1 = bf16[96,12288]{1,0:T(8,128)(2,1)} custom-call(f32[4,96,2048]{2,1,0:T(8,128)S(1)} %get-tuple-element.31.near_ref, f32[2,96,128]{2,1,0:T(8,128)S(1)} %get-tuple-element.32.value_ref, f32[2,128,128]{2,1,0:T(8,128)S(1)} %get-tuple-element.33.flip_ref, bf16[256,256]{1,0:T(8,128)(2,1)S(1)} %get-tuple-element.34.w_ref, ...), custom_call_target="tpu_custom_call" | custom-call | bytes 6000000 | tf_op jit(solution)/shard_map/update/pallas_call | solution.py:368
  (3 shorter events, 0.1 us)
Async XLA Ops:
  0.6 6.9 %copy-start.1 = (bf16[256,256]{1,0:T(8,128)(2,1)S(1)}, bf16[256,256]{1,0:T(8,128)(2,1)}, u32[]{:S(2)}) copy-start(bf16[256,256]{1,0:T(8,128)(2,1)} %constant.18.clone.w_hbm.w_ref) | copy-start | bytes 393220
  0.6 8.6 %copy-start = (bf16[256,256]{1,0:T(8,128)(2,1)S(1)}, bf16[256,256]{1,0:T(8,128)(2,1)}, u32[]{:S(2)}) copy-start(bf16[256,256]{1,0:T(8,128)(2,1)} %constant.19.clone.w_ref.w_hbm) | copy-start | bytes 393220
  4.2 4.8 %collective-permute-start = (f32[288,128]{1,0:T(8,128)S(1)}, f32[288,128]{1,0:T(8,128)S(1)}, u32[]{:S(2)}, u32[]{:S(2)}) collective-permute-start(f32[288,128]{1,0:T(8,128)S(1)} %bitcast.7), channel_id=1, source_target_pairs={{0,32},{32,0},{64,96},{96,64},{128,160},{160,128},{192,224},{224,1... | collective-permute-start | bytes 442376 | tf_op jit(solution)/shard_map/ppermute | solution.py:453
  9.1 4.1 %collective-permute-start.1 = (f32[288,128]{1,0:T(8,128)S(1)}, f32[288,128]{1,0:T(8,128)S(1)}, u32[]{:S(2)}, u32[]{:S(2)}) collective-permute-start(f32[288,128]{1,0:T(8,128)S(1)} %chip.1.after_ref.refs_0_), channel_id=1, source_target_pairs={{0,192},{32,96},{64,128},{96,32},{128,64},{160,224},{192,0},{224,1... | collective-permute-start | bytes 442376 | tf_op jit(solution)/shard_map/ppermute | solution.py:462
  13.2 5.3 %collective-permute-start.2 = (f32[288,128]{1,0:T(8,128)S(1)}, f32[288,128]{1,0:T(8,128)S(1)}, u32[]{:S(2)}, u32[]{:S(2)}) collective-permute-start(f32[288,128]{1,0:T(8,128)S(1)} %sum_0.1.after_ref.refs_0_), channel_id=1, source_target_pairs={{0,64},{32,224},{64,0},{96,160},{128,192},{160,96},{192,128},{224,... | collective-permute-start | bytes 442376 | tf_op jit(solution)/shard_map/ppermute | solution.py:462
  19.3 12.3 %collective-permute-start.3 = (f32[288,128]{1,0:T(8,128)S(1)}, f32[288,128]{1,0:T(8,128)S(1)}, u32[]{:S(2)}, u32[]{:S(2)}) collective-permute-start(f32[288,128]{1,0:T(8,128)S(1)} %get-tuple-element.30), channel_id=1, source_target_pairs={{0,32},{32,0},{64,96},{96,64},{128,160},{160,128},{192,224},{224,1... | collective-permute-start | bytes 442376 | tf_op jit(solution)/shard_map/ppermute | solution.py:504
  21.6 19.1 %all-to-all-start = ((f32[64,1,128]{2,1,0:T(1,128)}), f32[64,1,128]{2,1,0:T(1,128)S(1)}, u32[]{:S(2)}, u32[]{:S(2)}) async-start(f32[64,1,128]{2,1,0:T(1,128)} %get-tuple-element.35), calls=%async_computation | async-start | bytes 65536 | tf_op jit(solution)/shard_map/all_to_all | solution.py:503
  31.6 0.7 %copy-start.2 = (f32[288,128]{1,0:T(8,128)}, f32[288,128]{1,0:T(8,128)S(1)}, u32[]{:S(2)}) copy-start(f32[288,128]{1,0:T(8,128)S(1)} %collective-permute-done.3) | copy-start | bytes 442372

commit v7 on v6

--- a/solution.py
+++ b/solution.py
@@ -337,15 +337,21 @@
     def copy(g):
         return pltpu.make_async_copy(out_ref.at[g], out_hbm.at[:, columns(g)], sem.at[g])
 
-    for g in range(near):
+    early = near // 2
+    for g in range(early):
         out_ref[g] = (near_ref[g] * wide).astype(BF)
         copy(g).start()
 
     def store(i, t, part):
         if t is None:
+            for g in range(early, near) if i == 0 else ():
+                copy(g).start()
             copy(near + i).start()
         else:
-            out_ref[near + i, :, t * LANES : (t + 1) * LANES] = part.astype(BF)
+            here = slice(t * LANES, (t + 1) * LANES)
+            for g in range(early, near) if i == 0 else ():
+                out_ref[g, :, here] = (near_ref[g, :, here] * scale).astype(BF)
+            out_ref[near + i, :, here] = part.astype(BF)
 
     decode(
         groups - near, lambda i: flip_ref[i], lambda i: value_ref[i] * scale, w_ref,

time: 43.3 us -> 43.5 us (level)
  no operation moved by 1% of the time
where the time goes in v7:
time: 43.5 us; the launch traced here: 43.3 us
  Pallas kernels  16.9 us (39%)
  starting transfers between devices  16.8 us (39%)
  waiting for transfers between devices  8.03 us (18%)
  between operations  0.92 us (2%)
  local copies, waits for them, and re-layouts  0.67 us (2%)
    pallas_call x10, Pallas kernels, call(): pl.pallas_call(kernel, in_specs=specs, out_specs=outs if isinstance(out_s...  16.9 us
    all_to_all x1, starting transfers between devices, per_device(): energies = lax.all_to_all(own_energy, ('core',) + FSDP, 0, 0, tiled=True)  9.97 us
    all_to_all x1, waiting for transfers between devices, per_device(): energies = lax.all_to_all(own_energy, ('core',) + FSDP, 0, 0, tiled=True)  5.06 us
    ppermute x1, starting transfers between devices, per_device(): partner = lax.ppermute(other.reshape(flat), REP, swap)  3.33 us
    ppermute x2, waiting for transfers between devices, per_device(): arrived = [lax.ppermute(some, REP, pairs) for some in total]  2.96 us
    ppermute x1, starting transfers between devices, per_device(): total_other = lax.ppermute(total, REP, swap)  2.32 us
    ppermute x2, starting transfers between devices, per_device(): arrived = [lax.ppermute(some, REP, pairs) for some in total]  1.18 us
  transfers between devices with their start and end apart: 5, of which 3 were waited for; matrix products, arithmetic and copies ran while one was open for 0% of the time, Pallas kernels for 23%

profile of v7, /device:TPU:1, one launch (start us, length us, event | category | flops | bytes accessed | tf_op | source)
XLA Modules:
  0.0 43.3 jit_solution(3104837080491198390)
XLA Ops:
  0.6 0.0 copy-start.1
  0.6 0.0 copy-start
  0.7 3.6 %pick_other.1 = (s32[6,96,128]{2,1,0:T(8,128)S(1)}, f32[6,96,128]{2,1,0:T(8,128)S(1)}, f32[3,96,128]{2,1,0:T(8,128)S(1)}, f32[6,96,2048]{2,1,0:T(8,128)S(1)}) custom-call(s32[1]{0:T(128)} %bitcast.rep_ref, f32[1,96,12288]{2,1,0:T(8,128)} %x_hbm.1, s32[96,4,192]{2,1,0:T(4,128)} %bitcast.8, s32[8,96,192]{2,1,0:T(8,128)} %cnt_hbm.1, ...), custom_call_target="tpu_custom_call" | custom-call | bytes 12000000 | tf_op jit(solution)/shard_map/pick_other/pallas_call | solution.py:374
  4.2 3.3 %collective-permute-start = (f32[288,128]{1,0:T(8,128)S(1)}, f32[288,128]{1,0:T(8,128)S(1)}, u32[]{:S(2)}, u32[]{:S(2)}) collective-permute-start(f32[288,128]{1,0:T(8,128)S(1)} %bitcast.7), channel_id=1, source_target_pairs={{0,32},{32,0},{64,96},{96,64},{128,160},{160,128},{192,224},{224,1... | collective-permute-start | bytes 442376 | tf_op jit(solution)/shard_map/ppermute | solution.py:459
  7.6 0.0 copy-done.1
  7.6 1.5 %pick_mine.1.mine_ref = f32[3,96,128]{2,1,0:T(8,128)S(1)} custom-call(s32[1]{0:T(128)} %bitcast.rep_ref, f32[6,96,2048]{2,1,0:T(8,128)S(1)} %get-tuple-element.19.x_ref, s32[6,96,128]{2,1,0:T(8,128)S(1)} %get-tuple-element.20.number_ref.chosen_ref, f32[6,96,128]{2,1,0:T(8,128)S(1)} %get-tuple-element.21.live_ref, bf16[256,256]{1,0:T(8,128)(2,1)S(1)} %copy-done.1), custom_call_target="tpu_custom_call" | custom-call | bytes 6000000 | tf_op jit(solution)/shard_map/pick_mine/pallas_call | solution.py:374
  9.1 0.0 collective-permute-done.refs_1_
  9.1 0.1 collective-permute-start.1
  9.2 0.0 copy-done
  9.2 2.6 %residue_0.1 = (f32[1,96,12288]{2,1,0:T(8,128)}, f32[6,128,128]{2,1,0:T(8,128)}, f32[8,128]{1,0:T(8,128)S(1)}) custom-call(s32[1]{0:T(128)} %bitcast.rep_ref, f32[6,96,2048]{2,1,0:T(8,128)S(1)} %get-tuple-element.19.x_ref, s32[6,96,128]{2,1,0:T(8,128)S(1)} %get-tuple-element.20.number_ref.chosen_ref, f32[3,96,128]{2,1,0:T(8,128)S(1)} %pick_mine.1.mine_ref, ...), custom_call_target="tpu_custom_call" | custom-call | bytes 7500000 | tf_op jit(solution)/shard_map/residue_0/pallas_call | solution.py:374
  11.8 1.4 %collective-permute-done.1.refs_1_ = f32[288,128]{1,0:T(8,128)S(1)} collective-permute-done((f32[288,128]{1,0:T(8,128)S(1)}, f32[288,128]{1,0:T(8,128)S(1)}, u32[]{:S(2)}, u32[]{:S(2)}) %collective-permute-start.1) | collective-permute-done | bytes 147488 | tf_op jit(solution)/shard_map/ppermute | solution.py:468
  13.2 1.1 %collective-permute-start.2 = (f32[288,128]{1,0:T(8,128)S(1)}, f32[288,128]{1,0:T(8,128)S(1)}, u32[]{:S(2)}, u32[]{:S(2)}) collective-permute-start(f32[288,128]{1,0:T(8,128)S(1)} %sum_0.1.after_ref.refs_0_), channel_id=1, source_target_pairs={{0,64},{32,224},{64,0},{96,160},{128,192},{160,96},{192,128},{224,... | collective-permute-start | bytes 442376 | tf_op jit(solution)/shard_map/ppermute | solution.py:468
  14.3 2.6 %residue_1.1 = (f32[1,96,12288]{2,1,0:T(8,128)}, f32[6,128,128]{2,1,0:T(8,128)}, f32[8,128]{1,0:T(8,128)S(1)}) custom-call(s32[1]{0:T(128)} %bitcast.rep_ref, f32[6,96,2048]{2,1,0:T(8,128)S(1)} %get-tuple-element.19.x_ref, s32[6,96,128]{2,1,0:T(8,128)S(1)} %get-tuple-element.20.number_ref.chosen_ref, ...), custom_call_target="tpu_custom_call", output_to_operand_aliasing={{0}: (7, {}), {1}: (8, {})} | custom-call | bytes 7500000 | tf_op jit(solution)/shard_map/residue_1/pallas_call | solution.py:374
  16.9 1.6 %collective-permute-done.2.refs_1_ = f32[288,128]{1,0:T(8,128)S(1)} collective-permute-done((f32[288,128]{1,0:T(8,128)S(1)}, f32[288,128]{1,0:T(8,128)S(1)}, u32[]{:S(2)}, u32[]{:S(2)}) %collective-permute-start.2) | collective-permute-done | bytes 147488 | tf_op jit(solution)/shard_map/ppermute | solution.py:468
  18.5 0.7 %energy.1 = (f32[64,1,128]{2,1,0:T(1,128)}, f32[288,128]{1,0:T(8,128)S(1)}, f32[288,128]{1,0:T(8,128)}) custom-call(f32[288,128]{1,0:T(8,128)S(1)} %sum_1.1.total_ref), custom_call_target="tpu_custom_call" | custom-call | bytes 1500000 | tf_op jit(solution)/shard_map/energy/pallas_call | solution.py:374
  19.3 2.3 %collective-permute-start.3 = (f32[288,128]{1,0:T(8,128)S(1)}, f32[288,128]{1,0:T(8,128)S(1)}, u32[]{:S(2)}, u32[]{:S(2)}) collective-permute-start(f32[288,128]{1,0:T(8,128)S(1)} %get-tuple-element.30), channel_id=1, source_target_pairs={{0,32},{32,0},{64,96},{96,64},{128,160},{160,128},{192,224},{224,1... | collective-permute-start | bytes 442376 | tf_op jit(solution)/shard_map/ppermute | solution.py:510
  21.6 10.0 %all-to-all-start = ((f32[64,1,128]{2,1,0:T(1,128)}), f32[64,1,128]{2,1,0:T(1,128)S(1)}, u32[]{:S(2)}, u32[]{:S(2)}) async-start(f32[64,1,128]{2,1,0:T(1,128)} %get-tuple-element.35), calls=%async_computation | async-start | bytes 65536 | tf_op jit(solution)/shard_map/all_to_all | solution.py:509
  31.6 0.0 collective-permute-done.3
  31.6 0.0 copy-start.2
  31.6 0.7 %copy-done.2 = f32[288,128]{1,0:T(8,128)} copy-done((f32[288,128]{1,0:T(8,128)}, f32[288,128]{1,0:T(8,128)S(1)}, u32[]{:S(2)}) %copy-start.2) | copy-done | bytes 147480
  32.2 3.4 %raw.1 = (f32[4,96,2048]{2,1,0:T(8,128)S(1)}, f32[2,96,128]{2,1,0:T(8,128)S(1)}, f32[2,128,128]{2,1,0:T(8,128)S(1)}, bf16[256,256]{1,0:T(8,128)(2,1)S(1)}) custom-call(s32[1]{0:T(128)} %bitcast.rep_ref, f32[6,128,128]{2,1,0:T(8,128)} %get-tuple-element.27.flip_hbm, f32[3,96,128]{2,1,0:T(8,128)} %bitcast.9, f32[3,96,128]{2,1,0:T(8,128)} %bitcast.10, ...), custom_call_target="tpu_custom_call" | custom-call | bytes 15000000 | tf_op jit(solution)/shard_map/raw/pallas_call | solution.py:374
  35.6 5.1 %all-to-all-done.energy_ref = f32[64,1,128]{2,1,0:T(1,128)S(1)} async-done(((f32[64,1,128]{2,1,0:T(1,128)}), f32[64,1,128]{2,1,0:T(1,128)S(1)}, u32[]{:S(2)}, u32[]{:S(2)}) %all-to-all-start) | async-done | bytes 32800 | tf_op jit(solution)/shard_map/all_to_all | solution.py:509
  40.7 2.5 %update.1 = bf16[96,12288]{1,0:T(8,128)(2,1)} custom-call(f32[4,96,2048]{2,1,0:T(8,128)S(1)} %get-tuple-element.31.near_ref, f32[2,96,128]{2,1,0:T(8,128)S(1)} %get-tuple-element.32.value_ref, f32[2,128,128]{2,1,0:T(8,128)S(1)} %get-tuple-element.33.flip_ref, bf16[256,256]{1,0:T(8,128)(2,1)S(1)} %get-tuple-element.34.w_ref, ...), custom_call_target="tpu_custom_call" | custom-call | bytes 6000000 | tf_op jit(solution)/shard_map/update/pallas_call | solution.py:374
  (3 shorter events, 0.1 us)
Async XLA Ops:
  0.6 6.9 %copy-start.1 = (bf16[256,256]{1,0:T(8,128)(2,1)S(1)}, bf16[256,256]{1,0:T(8,128)(2,1)}, u32[]{:S(2)}) copy-start(bf16[256,256]{1,0:T(8,128)(2,1)} %constant.18.clone.w_hbm.w_ref) | copy-start | bytes 393220
  0.6 8.6 %copy-start = (bf16[256,256]{1,0:T(8,128)(2,1)S(1)}, bf16[256,256]{1,0:T(8,128)(2,1)}, u32[]{:S(2)}) copy-start(bf16[256,256]{1,0:T(8,128)(2,1)} %constant.19.clone.w_ref.w_hbm) | copy-start | bytes 393220
  4.2 4.8 %collective-permute-start = (f32[288,128]{1,0:T(8,128)S(1)}, f32[288,128]{1,0:T(8,128)S(1)}, u32[]{:S(2)}, u32[]{:S(2)}) collective-permute-start(f32[288,128]{1,0:T(8,128)S(1)} %bitcast.7), channel_id=1, source_target_pairs={{0,32},{32,0},{64,96},{96,64},{128,160},{160,128},{192,224},{224,1... | collective-permute-start | bytes 442376 | tf_op jit(solution)/shard_map/ppermute | solution.py:459
  9.1 4.1 %collective-permute-start.1 = (f32[288,128]{1,0:T(8,128)S(1)}, f32[288,128]{1,0:T(8,128)S(1)}, u32[]{:S(2)}, u32[]{:S(2)}) collective-permute-start(f32[288,128]{1,0:T(8,128)S(1)} %chip.1.after_ref.refs_0_), channel_id=1, source_target_pairs={{0,192},{32,96},{64,128},{96,32},{128,64},{160,224},{192,0},{224,1... | collective-permute-start | bytes 442376 | tf_op jit(solution)/shard_map/ppermute | solution.py:468
  13.2 5.3 %collective-permute-start.2 = (f32[288,128]{1,0:T(8,128)S(1)}, f32[288,128]{1,0:T(8,128)S(1)}, u32[]{:S(2)}, u32[]{:S(2)}) collective-permute-start(f32[288,128]{1,0:T(8,128)S(1)} %sum_0.1.after_ref.refs_0_), channel_id=1, source_target_pairs={{0,64},{32,224},{64,0},{96,160},{128,192},{160,96},{192,128},{224,... | collective-permute-start | bytes 442376 | tf_op jit(solution)/shard_map/ppermute | solution.py:468
  19.3 12.3 %collective-permute-start.3 = (f32[288,128]{1,0:T(8,128)S(1)}, f32[288,128]{1,0:T(8,128)S(1)}, u32[]{:S(2)}, u32[]{:S(2)}) collective-permute-start(f32[288,128]{1,0:T(8,128)S(1)} %get-tuple-element.30), channel_id=1, source_target_pairs={{0,32},{32,0},{64,96},{96,64},{128,160},{160,128},{192,224},{224,1... | collective-permute-start | bytes 442376 | tf_op jit(solution)/shard_map/ppermute | solution.py:510
  21.6 19.1 %all-to-all-start = ((f32[64,1,128]{2,1,0:T(1,128)}), f32[64,1,128]{2,1,0:T(1,128)S(1)}, u32[]{:S(2)}, u32[]{:S(2)}) async-start(f32[64,1,128]{2,1,0:T(1,128)} %get-tuple-element.35), calls=%async_computation | async-start | bytes 65536 | tf_op jit(solution)/shard_map/all_to_all | solution.py:509
  31.6 0.7 %copy-start.2 = (f32[288,128]{1,0:T(8,128)}, f32[288,128]{1,0:T(8,128)S(1)}, u32[]{:S(2)}) copy-start(f32[288,128]{1,0:T(8,128)S(1)} %collective-permute-done.3) | copy-start | bytes 442372
